TPU v7x, 32 devices: a whole 2x2x4 slice. The times are simulated.
32 devices in a mesh: dp: 8 (over z, x), tensor: 4 (over y, core).
Axes of the slice: x: 2, y: 2, z: 4, core: 2. Of those that a mesh axis runs over, the one named last changes fastest.
Arguments:
- tokens: bfloat16 [7680, 4096], P('dp'), may hold values from -70 to 70
- dense_weight: bfloat16 [4096, 14336], P('dp', 'tensor'), may hold values from -0.09375 to 0.09375
- left_factor: bfloat16 [64, 4096], P(None, 'tensor'), may hold values from -0.75 to 0.75
- right_factor: bfloat16 [64, 14336], P(None, 'tensor'), may hold values from -0.75 to 0.75
Outputs:
- dir_left: float32 [64, 4096], P('dp', 'tensor')
- dir_right: float32 [64, 14336], P('dp', 'tensor')
- loss: float32 [], replicated
All inputs are finite; a program needn't handle non-finite values.
Results may differ from a plain program's by a relative error of at most 0.0009.
Values may be sent and summed in bfloat16 or wider, within the bound.
No kernel may reach another device: no remote copies, remote signals or barrier semaphores. Data moves between devices by JAX's collectives and lax.ppermute only.
A program may use at most 128 MiB of HBM per device.

v0:
```python
import functools

import jax
import jax.numpy as jnp
from jax import lax
from jax.experimental import pallas as pl
from jax.experimental.pallas import tpu as pltpu
from jax.sharding import PartitionSpec as P

epsilon = 1e-06
VMEM_BYTES = 56 * 1024 * 1024


def swap(value, axis, stride):
    size = lax.axis_size(axis)
    return lax.ppermute(value, axis, [(a, a ^ stride) for a in range(size)])


def after(value, results):
    return lax.optimization_barrier((value, *results))[0] if results else value


def ordered(value, axis, strides):
    position = lax.axis_index(axis)
    for stride in strides:
        other = swap(value, axis, stride)
        high = (position // stride) % 2 == 1
        value = jnp.concatenate([jnp.where(high, other, value), jnp.where(high, value, other)], 0)
    return value


def contract(a, b, a_dim, b_dim):
    return lax.dot_general(a, b, (((a_dim,), (b_dim,)), ((), ())), preferred_element_type=jnp.float32)


AHEAD = 4


def row_tile(rows):
    return max(tile for tile in range(16, 513, 16) if rows % tile == 0)


def groups_of(low, high):
    cuts = [low, min(low + 2, high)] if low < high else [low]
    while cuts[-1] < high:
        cuts.append(min(cuts[-1] + 3, high))
    return list(zip(cuts[:-1], cuts[1:]))


def products_kernel(spans, parts, resumed, finish, blocks, scale, starts_ref, right_ref, *refs):
    count = len(parts)
    sets, refs = refs[: len(spans)], refs[len(spans) :]
    mixes, refs = refs[: len(spans)], refs[len(spans) :]
    pieces, refs = refs[: sum(parts)], refs[sum(parts) :]
    if resumed:
        partial_hbm, refs = refs[0], refs[1:]
    if finish:
        right_out, left_out, loss_out, total, rows_buf, mix_buf, piece_buf, sems, slope_buf, back_buf, turned_buf = refs
    else:
        total, rows_buf, mix_buf, piece_buf, sems = refs
    tokens = rows_buf.shape[0]
    depth = piece_buf.shape[0] // count
    slots = rows_buf.shape[1] // depth
    offsets = [sum(spans[:which]) for which in range(len(spans))]
    early = count - 2 if resumed else 0

    def start_of(slot):
        return pl.multiple_of(starts_ref[slot] * depth, depth)

    def copies(slot):
        found = []
        for which, span in enumerate(spans):
            target = rows_buf.at[pl.ds(offsets[which], span), pl.ds(slot * depth, depth)]
            source = sets[which].at[:, pl.ds(start_of(slot), depth)]
            found.append(pltpu.make_async_copy(source, target, sems.at[slot * len(spans) + which]))
        if slot < count:
            first, size = sum(parts[:slot]), depth // parts[slot]
            for part in range(parts[slot]):
                target = piece_buf.at[pl.ds(slot * depth + part * size, size)]
                sem = sems.at[(slots + 1) * len(spans) + 1 + first + part]
                found.append(pltpu.make_async_copy(pieces[first + part], target, sem))
        return found

    def begin(slots_now):
        for slot in slots_now:
            if slot < slots:
                for copy in copies(slot):
                    copy.start()

    def await_slots(slots_now):
        for slot in slots_now:
            for copy in copies(slot):
                copy.wait()

    def each_tile(low, high, body):
        if low < high:
            tile = row_tile(high - low)

            @pl.loop(0, (high - low) // tile)
            def _(step):
                body(pl.ds(pl.multiple_of(low + step * tile, 16), tile))

    first = [
        pltpu.make_async_copy(mixes[which], mix_buf.at[pl.ds(offsets[which], span)], sems.at[slots * len(spans) + which])
        for which, span in enumerate(spans)
    ]
    if resumed:
        sem = sems.at[(slots + 1) * len(spans)]
        first.append(pltpu.make_async_copy(partial_hbm, total.at[pl.ds(0, resumed)], sem))
    for copy in first:
        copy.start()
    begun = AHEAD
    begin(range(begun))
    for copy in first:
        copy.wait()
    for low, high in groups_of(0, early) + groups_of(early, count):
        begin(range(begun, high + AHEAD))
        begun = max(begun, high + AHEAD)
        await_slots(range(low, high))
        here = slice(low * depth, high * depth)

        def start_rows(at):
            term = contract(rows_buf[at, here], piece_buf[here], 1, 0)
            total[at] = contract(mix_buf[at], right_ref[...], 1, 0) - term

        def go_on(at):
            total[at] = total[at] - contract(rows_buf[at, here], piece_buf[here], 1, 0)

        if low < early:
            each_tile(resumed, tokens, go_on if low else start_rows)
        elif low:
            each_tile(0, resumed, go_on)
            each_tile(resumed, tokens, go_on)
        else:
            each_tile(0, tokens, start_rows)
    if not finish:
        return

    columns = right_ref.shape[1]
    mids = right_ref.shape[0] // blocks
    in_size = left_out.shape[1] // mids
    loss_out[...] = jnp.zeros_like(loss_out)
    begin(range(begun, slots))

    def slopes(at):
        residual = total[at]
        loss_out[...] += jnp.sum(residual * residual, axis=0, keepdims=True)
        slope = (residual * scale).astype(jnp.bfloat16)
        slope_buf[at] = slope
        back_buf[at] = contract(slope, right_ref[...], 1, 1)

    each_tile(0, tokens, slopes)
    full_right = contract(mix_buf[...], slope_buf[...], 0, 0)
    column_block = lax.broadcasted_iota(jnp.int32, (1, columns), 1) // (columns // blocks)
    grad_right = full_right[:mids]
    for b in range(1, blocks):
        grad_right = jnp.where(column_block == b, full_right[b * mids : (b + 1) * mids], grad_right)
    right_out[...] = grad_right
    turned_buf[...] = back_buf[...].T.astype(jnp.bfloat16)
    await_slots(range(count, slots))
    mid = lax.broadcasted_iota(jnp.int32, (mids, 1), 0)
    lane = lax.broadcasted_iota(jnp.int32, (1, depth), 1)

    @pl.loop(0, slots)
    def _(slot):
        full_left = contract(turned_buf[...], rows_buf[:, pl.ds(pl.multiple_of(slot * depth, depth), depth)], 1, 0)
        same = mid == (lane + start_of(slot)) // in_size
        sums = [
            jnp.sum(jnp.where(same, full_left[b * mids : (b + 1) * mids], 0.0), axis=0, keepdims=True)
            for b in range(blocks)
        ]
        left_out[:, pl.ds(start_of(slot), depth)] = jnp.concatenate(sums, 0)


def products(sets, mixes, right_diag, pieces, starts, blocks, scale, partial=None, finish=True):
    count = len(pieces)
    parts = tuple(len(piece) for piece in pieces)
    spans = tuple(rows.shape[0] for rows in sets)
    tokens, features = sum(spans), sets[0].shape[1]
    mid_columns, columns = right_diag.shape
    depth = sum(part.shape[0] for part in pieces[0])
    slots = starts.shape[0]
    resumed = 0 if partial is None else partial.shape[0]
    vmem = pl.BlockSpec(memory_space=pltpu.VMEM)
    operands = [starts, right_diag, *sets, *mixes, *[part for piece in pieces for part in piece]]
    if partial is not None:
        operands.append(partial)
    in_specs = [pl.BlockSpec(memory_space=pltpu.SMEM), vmem]
    in_specs += [pl.BlockSpec(memory_space=pl.ANY)] * (len(operands) - 2)
    scratch = [
        pltpu.VMEM((tokens, slots * depth), jnp.bfloat16),
        pltpu.VMEM((tokens, mid_columns), jnp.bfloat16),
        pltpu.VMEM((count * depth, columns), jnp.bfloat16),
        pltpu.SemaphoreType.DMA(((slots + 1) * len(spans) + 1 + sum(parts),)),
    ]
    flops = 2 * columns * depth * (tokens * count - resumed * (count - 2))
    if finish:
        shapes = [(mid_columns // blocks, columns), (blocks, features), (1, columns)]
        scratch = [pltpu.VMEM((tokens, columns), jnp.float32)] + scratch
        scratch += [
            pltpu.VMEM((tokens, columns), jnp.bfloat16),
            pltpu.VMEM((tokens, mid_columns), jnp.float32),
            pltpu.VMEM((mid_columns, tokens), jnp.bfloat16),
        ]
        flops += 4 * tokens * columns * mid_columns + 2 * tokens * mid_columns * features
    else:
        shapes = [(tokens, columns)]
    results = pl.pallas_call(
        functools.partial(products_kernel, spans, parts, resumed, finish, blocks, scale),
        out_shape=[jax.ShapeDtypeStruct(shape, jnp.float32) for shape in shapes],
        in_specs=in_specs,
        out_specs=[vmem] * len(shapes),
        scratch_shapes=scratch,
        compiler_params=pltpu.CompilerParams(vmem_limit_bytes=VMEM_BYTES),
        cost_estimate=pl.CostEstimate(
            flops=flops, bytes_accessed=2 * depth * (tokens * slots + columns * count), transcendentals=0
        ),
    )(*operands)
    return results if finish else results[0]


def mix_of(rows, left_diag):
    return jnp.dot(rows, left_diag, preferred_element_type=jnp.float32).astype(jnp.bfloat16)


def local(tokens, dense_weight, left_factor, right_factor):
    tok_rows, features = tokens.shape
    weight_rows, columns = dense_weight.shape
    dp_count = lax.axis_size("dp")
    tensor_count = lax.axis_size("tensor")
    dp_pos = lax.axis_index("dp")
    tensor_pos = lax.axis_index("tensor")
    in_size = left_factor.shape[0]
    mids = right_factor.shape[0]
    blocks = left_factor.shape[1] * tensor_count // mids
    own_blocks = blocks // tensor_count
    out_size = columns // own_blocks
    total_tokens = tok_rows * dp_count

    bits = dp_count.bit_length() - 1
    strides = [1 << b for b in range(bits)]
    grouped = max(bits - 3, 0)
    pair = strides[grouped:][len(strides[grouped:]) // 2]
    others = [s for s in reversed(strides[grouped:]) if s != pair]
    pair_bit = (dp_pos // pair) % 2
    unit_rows = weight_rows << grouped

    half_blocks = own_blocks // 2
    chunks = 2 if half_blocks % 2 == 0 else 1
    chunk_blocks = half_blocks // chunks
    chunk_columns = chunk_blocks * out_size
    half_columns = half_blocks * out_size

    def weight_piece(half, chunk, waits=()):
        start = half * half_columns + chunk * chunk_columns
        return lax.dynamic_slice_in_dim(after(dense_weight, waits), start, chunk_columns, 1)

    held = [{} for _ in range(chunks)]
    theirs = []
    for chunk in range(chunks):
        held[chunk][0] = ordered(weight_piece(pair_bit, chunk), "dp", strides[:grouped])
        theirs.append(ordered(weight_piece(1 - pair_bit, chunk), "dp", strides[:grouped]))
    far, near = others

    def send(chunk, mask, stride, waits=()):
        held[chunk][mask ^ stride] = swap(after(held[chunk][mask], waits), "dp", stride)
        return held[chunk][mask ^ stride]

    def send_pair(chunk, waits=()):
        held[chunk][pair] = swap(after(theirs[chunk], waits), "dp", pair)
        return held[chunk][pair]

    share = tok_rows // tensor_count
    first_cut = share * 7 // 15 // 16 * 16
    cuts = [0, first_cut, first_cut + (share - first_cut) // 2 // 16 * 16, share]

    def fetch_tokens(which, waits=()):
        begin, size = cuts[which], cuts[which + 1] - cuts[which]
        part = lax.dynamic_slice_in_dim(tokens, tensor_pos * share + begin, size, 0)
        return swap(after(part, waits), "dp", pair)

    def share_tokens(part, waits=()):
        stride = tensor_count // 2
        while stride:
            moved = swap(part, "tensor", stride)
            if stride == 1:
                return [part, moved]
            part = jnp.concatenate([part, after(moved, waits)], 0)
            stride, waits = stride // 2, ()
        return [part]

    last = chunks - 1
    parts = [None] * 2
    done = [send(0, 0, far), send_pair(0), send(0, 0, near)]
    if last:
        done.append(send(last, 0, near))
    first_done = done
    done = [send(0, pair, far, done), send(0, pair, near, done), send(0, far, near, done)] + (
        [send_pair(last, done)] if last else []
    )
    second_done = done

    left_blocks = after(left_factor, first_done).reshape(in_size, mids // tensor_count, blocks)
    left_blocks = lax.all_to_all(left_blocks, "tensor", split_axis=2, concat_axis=1, tiled=True)
    left_blocks = lax.dynamic_slice_in_dim(left_blocks, pair_bit * half_blocks, half_blocks, 2)
    eye_left = jnp.eye(mids, dtype=jnp.bfloat16)
    left_rows = left_blocks.transpose(1, 0, 2)
    left_diag = (left_rows[:, :, :, None] * eye_left[:, None, None, :]).reshape(features, half_blocks * mids)
    right_half = lax.dynamic_slice_in_dim(right_factor, pair_bit * half_columns, half_columns, 1)

    mixes = {0: mix_of(tokens, left_diag)}
    done = [*second_done, mixes[0]]
    parts[0] = fetch_tokens(0, done)
    done = [parts[0], send(0, far ^ pair, near, done)] + (
        [send(last, 0, far, done), send(last, pair, near, done)] if last else []
    )
    early_done = done

    row_block = jnp.arange(chunk_blocks * mids) // mids
    column_block = jnp.arange(chunk_columns) // out_size
    same_block = row_block[:, None] == column_block[None, :]

    token_sets = [tokens]
    order = [0, near, pair, far, far ^ near, pair ^ near, far ^ pair, far ^ pair ^ near]
    starts = jnp.stack([(dp_pos ^ mask) >> grouped for mask in order]).astype(jnp.int32)
    right_diags = []
    for chunk in range(chunks):
        right_chunk = right_half[:, chunk * chunk_columns : (chunk + 1) * chunk_columns]
        right_diags.append(jnp.where(same_block, jnp.tile(right_chunk, (chunk_blocks, 1)), jnp.bfloat16(0)))
    sums = [[] for _ in range(chunks)]
    halves = {}
    previous = None

    def run(which, chunk, end=len(order), partial=None, waits=()):
        nonlocal previous
        for item in which:
            if item not in mixes:
                mixes[item] = mix_of(token_sets[item], left_diag)
        waits = [*waits, *([] if previous is None else [previous])]
        mine = [mixes[item][:, chunk * chunk_blocks * mids : (chunk + 1) * chunk_blocks * mids] for item in which]
        mine[0] = after(mine[0], waits)
        pieces = [halves.get((chunk, mask), [held[chunk].get(mask)]) for mask in order[:end]]
        finish = end == len(order)
        terms = products(
            [token_sets[item] for item in which], mine, right_diags[chunk], pieces, starts[:end], chunk_blocks,
            1.0 / total_tokens, partial=partial, finish=finish,
        )
        if not finish:
            previous = terms
            return terms
        previous = terms[2]
        sums[chunk].append(terms)

    if last:
        source, cut = held[last][pair], unit_rows // 2
        upper = swap(after(source[:cut], early_done), "dp", far)
        late_part = fetch_tokens(1, early_done)
        near_part = send(last, far, near, early_done)
        run([0], 0, waits=early_done)
        token_sets += share_tokens(after(parts[0], early_done), [previous, upper, late_part, near_part])
        lower = swap(after(source[cut:], [upper]), "dp", far)
        last_part = fetch_tokens(2, [late_part])
        third_done = [lower, previous]
        early = list(range(1, len(token_sets)))
        run(early, 0)
        third_done.append(previous)
        parts[1] = jnp.concatenate([late_part, after(last_part, third_done)], 0)
        third_done.append(parts[1])
        fourth_done = [swap(after(half, third_done), "dp", near) for half in (upper, lower)]
        halves[last, far ^ pair] = [upper, lower]
        halves[last, far ^ pair ^ near] = fourth_done
        partial = run([0, *early], last, end=6)
        token_sets += share_tokens(after(parts[1], third_done), [partial, *fourth_done])
        late = list(range(len(early) + 1, len(token_sets)))
        mixes[late[0]] = mix_of(token_sets[late[0]], left_diag)
        run([0, *early], last, partial=partial, waits=[mixes[late[0]]])
        run(late, 0)
        run(late, last)
    else:
        for which in range(3):
            token_sets += share_tokens(fetch_tokens(which, early_done))
        run(range(len(token_sets)), 0)

    loss_part = 0.0
    summed = []
    for terms in sums:
        right_sum, left_sum = sum(term[0] for term in terms), sum(term[1] for term in terms)
        loss_part = loss_part + sum(jnp.sum(term[2]) for term in terms)
        left_sum = left_sum.reshape(chunk_blocks, mids, in_size).transpose(2, 0, 1).reshape(in_size, chunk_blocks * mids)
        both = jnp.concatenate([right_sum, left_sum], 1)
        both = both.reshape((2,) * bits + (both.shape[0] // dp_count, both.shape[1]))
        places = [s for s in reversed(strides)]
        for stride in [near, far] + strides[:grouped]:
            at = places.index(stride)
            bit = (dp_pos // stride) % 2
            away = lax.dynamic_index_in_dim(both, 1 - bit, at, keepdims=False)
            kept = lax.dynamic_index_in_dim(both, bit, at, keepdims=False)
            both = kept + swap(away, "dp", stride)
            places.remove(stride)
        summed.append(both)
    right_both = jnp.concatenate([both[..., :chunk_columns] for both in summed], -1)
    left_both = jnp.concatenate([both[..., chunk_columns:] for both in summed], -1)

    scalars = jnp.stack(
        [
            sum(jnp.sum(jnp.square(both[..., chunk_columns:])) for both in summed),
            sum(jnp.sum(jnp.square(both[..., :chunk_columns])) for both in summed),
            loss_part,
        ]
    )
    away = lax.dynamic_index_in_dim(right_both, 1 - pair_bit, 0, keepdims=False)
    kept = lax.dynamic_index_in_dim(right_both, pair_bit, 0, keepdims=False)
    other = swap(away, "dp", pair)
    right_rows = jnp.concatenate([jnp.where(pair_bit == 0, kept, other), jnp.where(pair_bit == 0, other, kept)], 1)

    rows_here = left_both.shape[1]
    left_both = left_both.reshape(2, rows_here, half_blocks, tensor_count, mids // tensor_count)
    left_both = left_both.transpose(0, 3, 1, 4, 2).reshape(2, tensor_count, -1)
    places = [dp_pos - pair_bit * pair, dp_pos + (1 - pair_bit) * pair]
    place = jnp.arange(dp_count)[:, None, None]
    outgoing = jnp.where(place == places[0], left_both[:1], jnp.where(place == places[1], left_both[1:], 0.0))
    scalars = jnp.pad(scalars, (0, 125))
    outgoing = jnp.concatenate([outgoing, jnp.broadcast_to(scalars, outgoing.shape[:2] + scalars.shape)], 2)
    incoming = lax.all_to_all(outgoing.reshape((-1,) + outgoing.shape[2:]), ("dp", "tensor"), 0, 0, tiled=True)
    sq_left, sq_right, loss_all = jnp.sum(incoming[:, -128:-125], 0)
    incoming = incoming[:, :-128].reshape(dp_count, tensor_count, rows_here, mids // tensor_count, half_blocks)
    left_both = jnp.stack([lax.dynamic_index_in_dim(incoming, p, 0, keepdims=False) for p in places])
    left_rows = left_both.transpose(2, 3, 1, 0, 4).reshape(rows_here, -1)
    dir_left = left_rows * lax.rsqrt(sq_left / (features * blocks) + epsilon)
    dir_right = right_rows * lax.rsqrt(sq_right / (mids * columns * tensor_count) + epsilon)
    loss = loss_all / (2.0 * total_tokens)
    return (dir_left, dir_right, loss)


def solution(mesh):
    in_specs = (P("dp", None), P("dp", "tensor"), P(None, "tensor"), P(None, "tensor"))
    out_specs = (P("dp", "tensor"), P("dp", "tensor"), P())
    return jax.shard_map(local, mesh=mesh, in_specs=in_specs, out_specs=out_specs, check_vma=False)
```

profile of v0, /device:TPU:0, one launch (start us, length us, event | category | flops | bytes accessed | tf_op | source)
XLA Modules:
  0.0 337.9 jit_solution(9248758295654251447)
XLA Ops:
  0.7 3.7 %constant_dynamic-slice_fusion.5 = (bf16[512,896]{1,0:T(8,128)(2,1)}, bf16[512,896]{1,0:T(8,128)(2,1)}, bf16[512,896]{1,0:T(8,128)(2,1)S(1)}, bf16[512,896]{1,0:T(8,128)(2,1)S(1)}) fusion(bf16[512,3584]{1,0:T(8,128)(2,1)} %param.5, s32[]{:T(128)S(6)} %select_n.147, s32[]{:T(128)S(6)} %select_n.143, s32[]{:T(128)S(6)} %select_n.141, s32[]{:T(128)S(6)} %select_n.144), kind=kLoop, calls=%fused_computation.72 | loop fusion | bytes 7340048 | tf_op jit(solution)/shard_map/dynamic_slice | solution.py:256
  4.4 3.0 collective-permute-start.1
  7.4 1.5 collective-permute-start.2
  8.9 2.6 collective-permute-start
  12.1 1.2 compare_select_fusion.1
  13.8 1.2 constant_dynamic-slice_fusion.6
  15.1 31.5 %collective-permute-done.1.refs_4_.refs_6_ = bf16[512,896]{1,0:T(8,128)(2,1)} collective-permute-done((bf16[512,896]{1,0:T(8,128)(2,1)}, bf16[512,896]{1,0:T(8,128)(2,1)}, u32[]{:S(2)}, u32[]{:S(2)}) %collective-permute-start.1) | collective-permute-done | bytes 917536 | tf_op jit(solution)/shard_map/ppermute | solution.py:16
  46.6 4.5 %collective-permute-done.refs_5_.refs_7_ = bf16[512,896]{1,0:T(8,128)(2,1)} collective-permute-done((bf16[512,896]{1,0:T(8,128)(2,1)S(1)}, bf16[512,896]{1,0:T(8,128)(2,1)}, u32[]{:S(2)}, u32[]{:S(2)}) %collective-permute-start) | collective-permute-done | bytes 917536 | tf_op jit(solution)/shard_map/ppermute | solution.py:16
  51.8 0.9 reshape.123
  52.6 3.3 all-to-all-start
  56.6 1.4 collective-permute-start.4
  58.5 2.6 collective-permute-start.7
  61.9 7.1 %broadcast_multiply_fusion = bf16[64,64,8,64]{3,2,1,0:T(8,128)(2,1)} fusion(bf16[64,64]{1,0:T(8,128)(2,1)S(1)} %fusion.16, bf16[64,64,8]{2,1,0:T(8,128)(2,1)S(1)} %copy.35), kind=kLoop, calls=%fused_computation | loop fusion | flops 2097152 | bytes 4268032 | tf_op jit(solution)/shard_map/mul | solution.py:308
  69.0 11.8 %mul.65 = bf16[4096,512]{1,0:T(8,128)(2,1)} reshape(bf16[64,64,8,64]{3,2,1,0:T(8,128)(2,1)} %broadcast_multiply_fusion) | data formatting | bytes 8388608 | tf_op jit(solution)/shard_map/mul | solution.py:308
  80.8 8.7 %fusion = bf16[960,512]{1,0:T(8,128)(2,1)S(1)} fusion(bf16[960,4096]{1,0:T(8,128)(2,1)} %refs_0_.5, bf16[4096,512]{1,0:T(8,128)(2,1)} %mul.65), kind=kOutput, calls=%fused_computation.2 | convolution fusion | flops 4027023360 | bytes 13041664 | tf_op jit(solution)/shard_map/dot_general | solution.py:223
  89.5 10.3 %collective-permute-done.4.refs_8_.refs_10_ = bf16[512,896]{1,0:T(8,128)(2,1)} collective-permute-done((bf16[512,896]{1,0:T(8,128)(2,1)}, bf16[512,896]{1,0:T(8,128)(2,1)}, u32[]{:S(2)}, u32[]{:S(2)}) %collective-permute-start.4) | collective-permute-done | bytes 917536 | tf_op jit(solution)/shard_map/ppermute | solution.py:16
  99.9 1.1 collective-permute-done.7.refs_8_.refs_6_
  101.7 2.0 collective-permute-start.10
  103.7 1.5 collective-permute-start.11
  105.2 1.3 constant_dynamic-slice_fusion.3
  106.5 1.0 fusion.20
  107.5 0.8 fusion.21
  108.3 32.2 %collective-permute-done.8 = bf16[112,4096]{1,0:T(8,128)(2,1)S(1)} collective-permute-done((bf16[112,4096]{1,0:T(8,128)(2,1)S(1)}, bf16[112,4096]{1,0:T(8,128)(2,1)S(1)}, u32[]{:S(2)}, u32[]{:S(2)}) %collective-permute-start.8) | collective-permute-done | bytes 917536 | tf_op jit(solution)/shard_map/ppermute | solution.py:16
  140.5 3.5 %collective-permute-done.10.refs_9_.refs_7_ = bf16[512,896]{1,0:T(8,128)(2,1)S(1)} collective-permute-done((bf16[512,896]{1,0:T(8,128)(2,1)S(1)}, bf16[512,896]{1,0:T(8,128)(2,1)S(1)}, u32[]{:S(2)}, u32[]{:S(2)}) %collective-permute-start.10) | collective-permute-done | bytes 917536 | tf_op jit(solution)/shard_map/ppermute | solution.py:16
  145.1 1.1 collective-permute-start.14
  146.2 1.7 collective-permute-start.12
  147.8 1.5 collective-permute-start.15
  149.3 19.2 %shard_map.67 = (f32[64,896]{1,0:T(8,128)}, f32[4,4096]{1,0:T(4,128)}, f32[1,896]{1,0:T(1,128)}) custom-call(s32[8]{0:T(128)} %stack.54.starts_ref, bf16[256,896]{1,0:T(8,128)(2,1)} %get-tuple-element.119.right_ref, bf16[960,4096]{1,0:T(8,128)(2,1)} %refs_0_.5, bf16[960,256]{1,0:T(8,128)(2,1)} %get-tuple-element.52.refs_1_, bf16[512,896]{1,0:T(8,128)(2,1)} %copy-done.4, ...), custom_call_target="tpu_custom_call" | custom-call | flops 9940500480 | bytes 15204352 | tf_op jit(solution)/shard_map/pallas_call | solution.py:208
  168.6 1.0 constant_dynamic-update-slice_fusion.1
  169.6 1.1 constant_dynamic-update-slice_fusion.refs_0_.refs_1_
  171.3 0.9 collective-permute-start.18
  172.2 1.0 collective-permute-start.17
  173.3 4.0 %convolution_convert_fusion.4 = bf16[224,512]{1,0:T(8,128)(2,1)S(1)} fusion(bf16[224,4096]{1,0:T(8,128)(2,1)} %constant_dynamic-update-slice_fusion.refs_0_.refs_1_, bf16[4096,512]{1,0:T(8,128)(2,1)} %mul.65), kind=kOutput, calls=%fused_computation.6 | convolution fusion | flops 939638784 | bytes 6258688 | tf_op jit(solution)/shard_map/dot_general | solution.py:223
  178.1 2.6 convolution_convert_fusion.3
  181.4 11.5 %shard_map.68 = (f32[64,896]{1,0:T(8,128)}, f32[4,4096]{1,0:T(4,128)}, f32[1,896]{1,0:T(1,128)}) custom-call(s32[8]{0:T(128)} %stack.54.starts_ref, bf16[256,896]{1,0:T(8,128)(2,1)} %get-tuple-element.119.right_ref, bf16[224,4096]{1,0:T(8,128)(2,1)} %constant_dynamic-update-slice_fusion.refs_0_.refs_1_, ...), custom_call_target="tpu_custom_call" | custom-call | flops 4638900224 | bytes 11010048 | tf_op jit(solution)/shard_map/pallas_call | solution.py:208
  193.0 1.5 collective-permute-done.18.refs_13_.refs_11_
  194.5 1.6 collective-permute-done.17
  196.2 0.9 collective-permute-start.20
  197.0 1.2 collective-permute-start.21
  198.6 17.8 %shard_map.69.refs_16_ = f32[1408,896]{1,0:T(8,128)} custom-call(s32[6]{0:T(128)} %stack.55.starts_ref, bf16[256,896]{1,0:T(8,128)(2,1)} %get-tuple-element.120.right_ref, bf16[960,4096]{1,0:T(8,128)(2,1)} %refs_0_.5, bf16[224,4096]{1,0:T(8,128)(2,1)} %constant_dynamic-update-slice_fusion.refs_0_.refs_1_, ...), custom_call_target="tpu_custom_call" | custom-call | flops 7751073792 | bytes 14155776 | tf_op jit(solution)/shard_map/pallas_call | solution.py:208
  216.6 1.6 collective-permute-done.21.refs_15_.refs_13_
  218.1 4.1 %collective-permute-done.19 = bf16[128,4096]{1,0:T(8,128)(2,1)S(1)} collective-permute-done((bf16[128,4096]{1,0:T(8,128)(2,1)S(1)}, bf16[128,4096]{1,0:T(8,128)(2,1)S(1)}, u32[]{:S(2)}, u32[]{:S(2)}) %collective-permute-start.19) | collective-permute-done | bytes 1048608 | tf_op jit(solution)/shard_map/ppermute | solution.py:16
  225.4 3.4 %convolution_convert_fusion.2 = bf16[256,512]{1,0:T(8,128)(2,1)S(1)} fusion(bf16[256,4096]{1,0:T(8,128)(2,1)S(1)} %constant_dynamic-update-slice_fusion.4.refs_0_, bf16[4096,512]{1,0:T(8,128)(2,1)} %mul.65), kind=kOutput, calls=%fused_computation.4 | convolution fusion | flops 1073872896 | bytes 6553600 | tf_op jit(solution)/shard_map/dot_general | solution.py:223
  228.9 31.1 %shard_map.70 = (f32[64,896]{1,0:T(8,128)}, f32[4,4096]{1,0:T(4,128)}, f32[1,896]{1,0:T(1,128)}) custom-call(s32[8]{0:T(128)} %stack.54.starts_ref, bf16[256,896]{1,0:T(8,128)(2,1)} %get-tuple-element.120.right_ref, bf16[960,4096]{1,0:T(8,128)(2,1)} %refs_0_.5, bf16[224,4096]{1,0:T(8,128)(2,1)} %constant_dynamic-update-slice_fusion.refs_0_.refs_1_, ...), custom_call_target="tpu_custom_call" | custom-call | flops 6828326912 | bytes 18874368 | tf_op jit(solution)/shard_map/pallas_call | solution.py:208
  260.0 1.4 reduce_sum.97
  261.4 0.7 fusion.24
  262.1 4.1 %convolution_convert_fusion.1 = bf16[256,512]{1,0:T(8,128)(2,1)S(1)} fusion(bf16[256,4096]{1,0:T(8,128)(2,1)} %collective-permute-done.22.refs_1_, bf16[4096,512]{1,0:T(8,128)(2,1)} %mul.65), kind=kOutput, calls=%fused_computation.3 | convolution fusion | flops 1073872896 | bytes 6553600 | tf_op jit(solution)/shard_map/dot_general | solution.py:223
  266.2 0.7 fusion.23
  266.9 12.1 %shard_map.71 = (f32[64,896]{1,0:T(8,128)}, f32[4,4096]{1,0:T(4,128)}, f32[1,896]{1,0:T(1,128)}) custom-call(s32[8]{0:T(128)} %stack.54.starts_ref, bf16[256,896]{1,0:T(8,128)(2,1)} %get-tuple-element.119.right_ref, bf16[256,4096]{1,0:T(8,128)(2,1)} %copy-done.5, bf16[256,4096]{1,0:T(8,128)(2,1)} %collective-permute-done.22.refs_1_, ...), custom_call_target="tpu_custom_call" | custom-call | flops 5301600256 | bytes 11534336 | tf_op jit(solution)/shard_map/pallas_call | solution.py:208
  279.0 1.3 reduce_sum.96
  280.4 12.2 %shard_map.72 = (f32[64,896]{1,0:T(8,128)}, f32[4,4096]{1,0:T(4,128)}, f32[1,896]{1,0:T(1,128)}) custom-call(s32[8]{0:T(128)} %stack.54.starts_ref, bf16[256,896]{1,0:T(8,128)(2,1)} %get-tuple-element.120.right_ref, bf16[256,4096]{1,0:T(8,128)(2,1)} %copy-done.5, bf16[256,4096]{1,0:T(8,128)(2,1)} %collective-permute-done.22.refs_1_, ...), custom_call_target="tpu_custom_call" | custom-call | flops 5301600256 | bytes 11534336 | tf_op jit(solution)/shard_map/pallas_call | solution.py:208
  292.6 1.3 reduce_sum.98
  293.9 0.9 add.192
  295.6 1.0 add.191
  296.6 1.4 collective-permute-start.25
  298.1 0.7 collective-permute-start.23
  300.7 2.6 collective-permute-done.25
  304.0 1.9 collective-permute-done.23
  306.6 4.9 %collective-permute-done.26 = f32[2,8,1152]{2,1,0:T(8,128)S(1)} collective-permute-done((f32[2,8,1152]{2,1,0:T(8,128)S(1)}, f32[2,8,1152]{2,1,0:T(8,128)S(1)}, u32[]{:S(2)}, u32[]{:S(2)}) %collective-permute-start.26) | collective-permute-done | bytes 73760 | tf_op jit(solution)/shard_map/ppermute | solution.py:16
  317.8 0.8 all_to_all.25
  318.5 3.3 all-to-all-start.1
  321.8 8.4 %all-to-all-done.1 = f32[32,1,1152]{2,1,0:T(1,128)S(1)} async-done(((f32[32,1,1152]{2,1,0:T(1,128)}), f32[32,1,1152]{2,1,0:T(1,128)S(1)}, u32[]{:S(2)}, u32[]{:S(2)}) %all-to-all-start.1) | async-done | bytes 147488 | tf_op jit(solution)/shard_map/all_to_all | solution.py:424
  332.2 1.1 reshape.121
  333.9 1.4 mul.71
  (151 shorter events, 17.4 us)
Async XLA Ops:
  0.7 11.4 %copy-start.12 = (bf16[64,3584]{1,0:T(8,128)(2,1)S(1)}, bf16[64,3584]{1,0:T(8,128)(2,1)}, u32[]{:S(2)}) copy-start(bf16[64,3584]{1,0:T(8,128)(2,1)} %param.7) | copy-start | bytes 1376260
  0.7 50.5 %copy-start.11 = (bf16[64,1024]{1,0:T(8,128)(2,1)S(1)}, bf16[64,1024]{1,0:T(8,128)(2,1)}, u32[]{:S(2)}) copy-start(bf16[64,1024]{1,0:T(8,128)(2,1)} %param.6) | copy-start | bytes 393220
  4.4 46.8 %copy-start.2 = (bf16[512,896]{1,0:T(8,128)(2,1)}, bf16[512,896]{1,0:T(8,128)(2,1)S(1)}, u32[]{:S(2)}) copy-start(bf16[512,896]{1,0:T(8,128)(2,1)S(1)} %get-tuple-element.50.refs_6_.refs_4_) | copy-start | bytes 2752516
  4.4 53.6 %copy-start.4 = (bf16[512,896]{1,0:T(8,128)(2,1)}, bf16[512,896]{1,0:T(8,128)(2,1)S(1)}, u32[]{:S(2)}) copy-start(bf16[512,896]{1,0:T(8,128)(2,1)S(1)} %get-tuple-element.89.refs_2_.refs_4_) | copy-start | bytes 2752516
  4.4 42.2 %collective-permute-start.1 = (bf16[512,896]{1,0:T(8,128)(2,1)}, bf16[512,896]{1,0:T(8,128)(2,1)}, u32[]{:S(2)}, u32[]{:S(2)}) collective-permute-start(bf16[512,896]{1,0:T(8,128)(2,1)} %get-tuple-element.88), channel_id=1, source_target_pairs={{0,8},{4,12},{8,0},{12,4},{16,24},{20,28},{24,16},{28,20},{1,9},{5... | collective-permute-start | bytes 2752520 | tf_op jit(solution)/shard_map/ppermute | solution.py:16
  7.4 39.2 %collective-permute-start.2 = (bf16[512,896]{1,0:T(8,128)(2,1)S(1)}, bf16[512,896]{1,0:T(8,128)(2,1)}, u32[]{:S(2)}, u32[]{:S(2)}) collective-permute-start(bf16[512,896]{1,0:T(8,128)(2,1)S(1)} %get-tuple-element.89.refs_2_.refs_4_), channel_id=1, source_target_pairs={{0,4},{4,0},{8,12},{12,8},{16,20},{20,16},{24,28},{28,24},{1,5},{5... | collective-permute-start | bytes 2752520 | tf_op jit(solution)/shard_map/ppermute | solution.py:16
  8.9 42.2 %collective-permute-start = (bf16[512,896]{1,0:T(8,128)(2,1)S(1)}, bf16[512,896]{1,0:T(8,128)(2,1)}, u32[]{:S(2)}, u32[]{:S(2)}) collective-permute-start(bf16[512,896]{1,0:T(8,128)(2,1)S(1)} %get-tuple-element.89.refs_2_.refs_4_), channel_id=1, source_target_pairs={{0,16},{4,20},{8,24},{12,28},{16,0},{20,4},{24,8},{28,12},{1,17},{... | collective-permute-start | bytes 2752520 | tf_op jit(solution)/shard_map/ppermute | solution.py:16
  11.5 39.7 %collective-permute-start.3 = (bf16[512,896]{1,0:T(8,128)(2,1)S(1)}, bf16[512,896]{1,0:T(8,128)(2,1)}, u32[]{:S(2)}, u32[]{:S(2)}) collective-permute-start(bf16[512,896]{1,0:T(8,128)(2,1)S(1)} %get-tuple-element.50.refs_6_.refs_4_), channel_id=1, source_target_pairs={{0,4},{4,0},{8,12},{12,8},{16,20},{20,16},{24,28},{28,24},{1,5},{5... | collective-permute-start | bytes 2752520 | tf_op jit(solution)/shard_map/ppermute | solution.py:16
  52.6 8.5 %all-to-all-start = ((bf16[4,2,8192]{2,1,0:T(2,128)(2,1)}), bf16[4,2,8192]{2,1,0:T(2,128)(2,1)S(1)}, u32[]{:S(2)}, u32[]{:S(2)}) async-start(bf16[4,2,8192]{2,1,0:T(2,128)(2,1)} %reshape.123), calls=%async_computation | async-start | bytes 262144 | tf_op jit(solution)/shard_map/all_to_all | solution.py:304
  56.0 33.5 %collective-permute-start.5 = (bf16[512,896]{1,0:T(8,128)(2,1)}, bf16[512,896]{1,0:T(8,128)(2,1)}, u32[]{:S(2)}, u32[]{:S(2)}) collective-permute-start(bf16[512,896]{1,0:T(8,128)(2,1)} %collective-permute-done.1.refs_4_.refs_6_), channel_id=1, source_target_pairs={{0,4},{4,0},{8,12},{12,8},{16,20},{20,16},{24,28},{28,24},{1,5},{5... | collective-permute-start | bytes 2752520 | tf_op jit(solution)/shard_map/ppermute | solution.py:16
  56.6 43.3 %collective-permute-start.4 = (bf16[512,896]{1,0:T(8,128)(2,1)}, bf16[512,896]{1,0:T(8,128)(2,1)}, u32[]{:S(2)}, u32[]{:S(2)}) collective-permute-start(bf16[512,896]{1,0:T(8,128)(2,1)} %collective-permute-done.1.refs_4_.refs_6_), channel_id=1, source_target_pairs={{0,16},{4,20},{8,24},{12,28},{16,0},{20,4},{24,8},{28,12},{1,17},{... | collective-permute-start | bytes 2752520 | tf_op jit(solution)/shard_map/ppermute | solution.py:16
  58.0 41.9 %collective-permute-start.6 = (bf16[512,896]{1,0:T(8,128)(2,1)}, bf16[512,896]{1,0:T(8,128)(2,1)}, u32[]{:S(2)}, u32[]{:S(2)}) collective-permute-start(bf16[512,896]{1,0:T(8,128)(2,1)} %collective-permute-done.refs_5_.refs_7_), channel_id=1, source_target_pairs={{0,4},{4,0},{8,12},{12,8},{16,20},{20,16},{24,28},{28,24},{1,5},{5... | collective-permute-start | bytes 2752520 | tf_op jit(solution)/shard_map/ppermute | solution.py:16
  58.5 42.5 %collective-permute-start.7 = (bf16[512,896]{1,0:T(8,128)(2,1)}, bf16[512,896]{1,0:T(8,128)(2,1)S(1)}, u32[]{:S(2)}, u32[]{:S(2)}) collective-permute-start(bf16[512,896]{1,0:T(8,128)(2,1)} %get-tuple-element.47), channel_id=1, source_target_pairs={{0,8},{4,12},{8,0},{12,4},{16,24},{20,28},{24,16},{28,20},{1,9},{5... | collective-permute-start | bytes 2752520 | tf_op jit(solution)/shard_map/ppermute | solution.py:16
  80.8 20.9 %copy-start.3 = (bf16[512,896]{1,0:T(8,128)(2,1)S(1)}, bf16[512,896]{1,0:T(8,128)(2,1)}, u32[]{:S(2)}) copy-start(bf16[512,896]{1,0:T(8,128)(2,1)} %copy-done.2) | copy-start | bytes 2752516
  101.0 67.5 %copy-start.1 = (bf16[512,896]{1,0:T(8,128)(2,1)}, bf16[512,896]{1,0:T(8,128)(2,1)S(1)}, u32[]{:S(2)}) copy-start(bf16[512,896]{1,0:T(8,128)(2,1)S(1)} %collective-permute-done.7.refs_8_.refs_6_) | copy-start | bytes 2752516
  101.0 39.5 %collective-permute-start.8 = (bf16[112,4096]{1,0:T(8,128)(2,1)S(1)}, bf16[112,4096]{1,0:T(8,128)(2,1)S(1)}, u32[]{:S(2)}, u32[]{:S(2)}) collective-permute-start(bf16[112,4096]{1,0:T(8,128)(2,1)S(1)} %constant_dynamic-slice_fusion.6), channel_id=1, source_target_pairs={{0,8},{4,12},{8,0},{12,4},{16,24},{20,28},{24,16},{28,20},{1,9},{5... | collective-permute-start | bytes 2752520 | tf_op jit(solution)/shard_map/ppermute | solution.py:16
  101.0 39.5 %collective-permute-start.9 = (bf16[512,896]{1,0:T(8,128)(2,1)}, bf16[512,896]{1,0:T(8,128)(2,1)S(1)}, u32[]{:S(2)}, u32[]{:S(2)}) collective-permute-start(bf16[512,896]{1,0:T(8,128)(2,1)} %collective-permute-done.4.refs_8_.refs_10_), channel_id=1, source_target_pairs={{0,4},{4,0},{8,12},{12,8},{16,20},{20,16},{24,28},{28,24},{1,5},{5... | collective-permute-start | bytes 2752520 | tf_op jit(solution)/shard_map/ppermute | solution.py:16
  101.7 42.4 %collective-permute-start.10 = (bf16[512,896]{1,0:T(8,128)(2,1)S(1)}, bf16[512,896]{1,0:T(8,128)(2,1)S(1)}, u32[]{:S(2)}, u32[]{:S(2)}) collective-permute-start(bf16[512,896]{1,0:T(8,128)(2,1)S(1)} %copy-done.3), channel_id=1, source_target_pairs={{0,16},{4,20},{8,24},{12,28},{16,0},{20,4},{24,8},{28,12},{1,17},{... | collective-permute-start | bytes 2752520 | tf_op jit(solution)/shard_map/ppermute | solution.py:16
  103.7 40.4 %collective-permute-start.11 = (bf16[512,896]{1,0:T(8,128)(2,1)S(1)}, bf16[512,896]{1,0:T(8,128)(2,1)S(1)}, u32[]{:S(2)}, u32[]{:S(2)}) collective-permute-start(bf16[512,896]{1,0:T(8,128)(2,1)S(1)} %collective-permute-done.7.refs_8_.refs_6_), channel_id=1, source_target_pairs={{0,4},{4,0},{8,12},{12,8},{16,20},{20,16},{24,28},{28,24},{1,5},{5... | collective-permute-start | bytes 2752520 | tf_op jit(solution)/shard_map/ppermute | solution.py:16
  140.5 8.8 %copy-start.21 = (bf16[512,896]{1,0:T(8,128)(2,1)}, bf16[512,896]{1,0:T(8,128)(2,1)S(1)}, u32[]{:S(2)}) copy-start(bf16[512,896]{1,0:T(8,128)(2,1)S(1)} %collective-permute-done.9.refs_9_.refs_11_) | copy-start | bytes 2752516
  144.1 24.4 %copy-start.19 = (bf16[512,896]{1,0:T(8,128)(2,1)}, bf16[512,896]{1,0:T(8,128)(2,1)S(1)}, u32[]{:S(2)}) copy-start(bf16[512,896]{1,0:T(8,128)(2,1)S(1)} %collective-permute-done.10.refs_9_.refs_7_) | copy-start | bytes 2752516
  144.1 1.0 copy-start.20
  144.1 25.5 %collective-permute-start.13 = (bf16[256,896]{1,0:T(8,128)(2,1)S(1)}, bf16[256,896]{1,0:T(8,128)(2,1)}, u32[]{:S(2)}, u32[]{:S(2)}) collective-permute-start(bf16[256,896]{1,0:T(8,128)(2,1)S(1)} %get-tuple-element.56), channel_id=1, source_target_pairs={{0,16},{4,20},{8,24},{12,28},{16,0},{20,4},{24,8},{28,12},{1,17},{... | collective-permute-start | bytes 1376264 | tf_op jit(solution)/shard_map/ppermute | solution.py:16
  145.1 24.5 %collective-permute-start.14 = (bf16[64,4096]{1,0:T(8,128)(2,1)S(1)}, bf16[64,4096]{1,0:T(8,128)(2,1)S(1)}, u32[]{:S(2)}, u32[]{:S(2)}) collective-permute-start(bf16[64,4096]{1,0:T(8,128)(2,1)S(1)} %get-tuple-element.57), channel_id=1, source_target_pairs={{0,8},{4,12},{8,0},{12,4},{16,24},{20,28},{24,16},{28,20},{1,9},{5... | collective-permute-start | bytes 1572872 | tf_op jit(solution)/shard_map/ppermute | solution.py:16
  146.2 23.4 %collective-permute-start.12 = (bf16[112,4096]{1,0:T(8,128)(2,1)S(1)}, bf16[112,4096]{1,0:T(8,128)(2,1)S(1)}, u32[]{:S(2)}, u32[]{:S(2)}) collective-permute-start(bf16[112,4096]{1,0:T(8,128)(2,1)S(1)} %collective-permute-done.8), channel_id=1, source_target_pairs={{0,2},{1,3},{2,0},{3,1},{4,6},{5,7},{6,4},{7,5},{8,10},{9,11},{10,... | collective-permute-start | bytes 2752520 | tf_op jit(solution)/shard_map/ppermute | solution.py:16
  147.8 21.7 %collective-permute-start.15 = (bf16[512,896]{1,0:T(8,128)(2,1)S(1)}, bf16[512,896]{1,0:T(8,128)(2,1)S(1)}, u32[]{:S(2)}, u32[]{:S(2)}) collective-permute-start(bf16[512,896]{1,0:T(8,128)(2,1)S(1)} %collective-permute-done.10.refs_9_.refs_7_), channel_id=1, source_target_pairs={{0,4},{4,0},{8,12},{12,8},{16,20},{20,16},{24,28},{28,24},{1,5},{5... | collective-permute-start | bytes 2752520 | tf_op jit(solution)/shard_map/ppermute | solution.py:16
  168.6 2.8 copy-start.6
  169.6 7.8 %copy-start.22 = (bf16[512,896]{1,0:T(8,128)(2,1)}, bf16[512,896]{1,0:T(8,128)(2,1)S(1)}, u32[]{:S(2)}) copy-start(bf16[512,896]{1,0:T(8,128)(2,1)S(1)} %collective-permute-done.15.refs_10_.refs_8_) | copy-start | bytes 2752516
  170.7 7.4 %collective-permute-start.16 = (bf16[224,4096]{1,0:T(8,128)(2,1)}, bf16[224,4096]{1,0:T(8,128)(2,1)}, u32[]{:S(2)}, u32[]{:S(2)}) collective-permute-start(bf16[224,4096]{1,0:T(8,128)(2,1)} %constant_dynamic-update-slice_fusion.refs_0_.refs_1_), channel_id=1, source_target_pairs={{0,1},{1,0},{2,3},{3,2},{4,5},{5,4},{6,7},{7,6},{8,9},{9,8},{10,11... | collective-permute-start | bytes 5505032 | tf_op jit(solution)/shard_map/ppermute | solution.py:16
  171.3 23.2 %collective-permute-start.18 = (bf16[256,896]{1,0:T(8,128)(2,1)S(1)}, bf16[256,896]{1,0:T(8,128)(2,1)S(1)}, u32[]{:S(2)}, u32[]{:S(2)}) collective-permute-start(bf16[256,896]{1,0:T(8,128)(2,1)S(1)} %copy-done.6), channel_id=1, source_target_pairs={{0,16},{4,20},{8,24},{12,28},{16,0},{20,4},{24,8},{28,12},{1,17},{... | collective-permute-start | bytes 1376264 | tf_op jit(solution)/shard_map/ppermute | solution.py:16
  172.2 23.9 %collective-permute-start.17 = (bf16[64,4096]{1,0:T(8,128)(2,1)S(1)}, bf16[64,4096]{1,0:T(8,128)(2,1)S(1)}, u32[]{:S(2)}, u32[]{:S(2)}) collective-permute-start(bf16[64,4096]{1,0:T(8,128)(2,1)S(1)} %get-tuple-element.62), channel_id=1, source_target_pairs={{0,8},{4,12},{8,0},{12,4},{16,24},{20,28},{24,16},{28,20},{1,9},{5... | collective-permute-start | bytes 1572872 | tf_op jit(solution)/shard_map/ppermute | solution.py:16
  173.3 4.7 %copy-start = (bf16[4096,512]{1,0:T(8,128)(2,1)S(1)}, bf16[4096,512]{1,0:T(8,128)(2,1)}, u32[]{:S(2)}) copy-start(bf16[4096,512]{1,0:T(8,128)(2,1)} %mul.65) | copy-start | bytes 12582916
  194.5 21.9 %copy-start.23 = (bf16[256,896]{1,0:T(8,128)(2,1)}, bf16[256,896]{1,0:T(8,128)(2,1)S(1)}, u32[]{:S(2)}) copy-start(bf16[256,896]{1,0:T(8,128)(2,1)S(1)} %collective-permute-done.18.refs_13_.refs_11_) | copy-start | bytes 1376260
  196.2 20.4 %collective-permute-start.20 = (bf16[256,896]{1,0:T(8,128)(2,1)}, bf16[256,896]{1,0:T(8,128)(2,1)S(1)}, u32[]{:S(2)}, u32[]{:S(2)}) collective-permute-start(bf16[256,896]{1,0:T(8,128)(2,1)} %collective-permute-done.13.refs_12_.refs_10_), channel_id=1, source_target_pairs={{0,4},{4,0},{8,12},{12,8},{16,20},{20,16},{24,28},{28,24},{1,5},{5... | collective-permute-start | bytes 1376264 | tf_op jit(solution)/shard_map/ppermute | solution.py:16
  197.0 21.1 %collective-permute-start.21 = (bf16[256,896]{1,0:T(8,128)(2,1)S(1)}, bf16[256,896]{1,0:T(8,128)(2,1)S(1)}, u32[]{:S(2)}, u32[]{:S(2)}) collective-permute-start(bf16[256,896]{1,0:T(8,128)(2,1)S(1)} %collective-permute-done.18.refs_13_.refs_11_), channel_id=1, source_target_pairs={{0,4},{4,0},{8,12},{12,8},{16,20},{20,16},{24,28},{28,24},{1,5},{5... | collective-permute-start | bytes 1376264 | tf_op jit(solution)/shard_map/ppermute | solution.py:16
  198.2 24.0 %collective-permute-start.19 = (bf16[128,4096]{1,0:T(8,128)(2,1)S(1)}, bf16[128,4096]{1,0:T(8,128)(2,1)S(1)}, u32[]{:S(2)}, u32[]{:S(2)}) collective-permute-start(bf16[128,4096]{1,0:T(8,128)(2,1)S(1)} %constant_dynamic-update-slice_fusion.2), channel_id=1, source_target_pairs={{0,2},{1,3},{2,0},{3,1},{4,6},{5,7},{6,4},{7,5},{8,10},{9,11},{10,... | collective-permute-start | bytes 3145736 | tf_op jit(solution)/shard_map/ppermute | solution.py:16
  216.4 6.4 %copy-start.17 = (f32[1,896]{1,0:T(1,128)S(1)}, f32[1,896]{1,0:T(1,128)}, u32[]{:S(2)}) copy-start(f32[1,896]{1,0:T(1,128)} %get-tuple-element.55) | copy-start | bytes 10756
  216.4 7.1 %copy-start.18 = (f32[1,896]{1,0:T(1,128)S(1)}, f32[1,896]{1,0:T(1,128)}, u32[]{:S(2)}) copy-start(f32[1,896]{1,0:T(1,128)} %get-tuple-element.64) | copy-start | bytes 10756
  216.5 12.3 %copy-start.24 = (bf16[256,896]{1,0:T(8,128)(2,1)}, bf16[256,896]{1,0:T(8,128)(2,1)S(1)}, u32[]{:S(2)}) copy-start(bf16[256,896]{1,0:T(8,128)(2,1)S(1)} %collective-permute-done.20.refs_14_.refs_12_) | copy-start | bytes 1376260
  218.1 10.7 %copy-start.25 = (bf16[256,896]{1,0:T(8,128)(2,1)}, bf16[256,896]{1,0:T(8,128)(2,1)S(1)}, u32[]{:S(2)}) copy-start(bf16[256,896]{1,0:T(8,128)(2,1)S(1)} %collective-permute-done.21.refs_15_.refs_13_) | copy-start | bytes 1376260
  222.3 6.6 %copy-start.5 = (bf16[256,4096]{1,0:T(8,128)(2,1)}, bf16[256,4096]{1,0:T(8,128)(2,1)S(1)}, u32[]{:S(2)}) copy-start(bf16[256,4096]{1,0:T(8,128)(2,1)S(1)} %constant_dynamic-update-slice_fusion.4.refs_0_) | copy-start | bytes 6291460
  222.3 39.8 %collective-permute-start.22 = (bf16[256,4096]{1,0:T(8,128)(2,1)S(1)}, bf16[256,4096]{1,0:T(8,128)(2,1)}, u32[]{:S(2)}, u32[]{:S(2)}) collective-permute-start(bf16[256,4096]{1,0:T(8,128)(2,1)S(1)} %constant_dynamic-update-slice_fusion.4.refs_0_), channel_id=1, source_target_pairs={{0,1},{1,0},{2,3},{3,2},{4,5},{5,4},{6,7},{7,6},{8,9},{9,8},{10,11... | collective-permute-start | bytes 6291464 | tf_op jit(solution)/shard_map/ppermute | solution.py:16
  280.3 13.6 %copy-start.13 = (f32[4,4096]{1,0:T(4,128)S(1)}, f32[4,4096]{1,0:T(4,128)}, u32[]{:S(2)}) copy-start(f32[4,4096]{1,0:T(4,128)} %get-tuple-element.82) | copy-start | bytes 196612
  280.3 14.8 %copy-start.14 = (f32[4,4096]{1,0:T(4,128)S(1)}, f32[4,4096]{1,0:T(4,128)}, u32[]{:S(2)}) copy-start(f32[4,4096]{1,0:T(4,128)} %get-tuple-element.75) | copy-start | bytes 196612
  280.3 14.8 %copy-start.15 = (f32[4,4096]{1,0:T(4,128)S(1)}, f32[4,4096]{1,0:T(4,128)}, u32[]{:S(2)}) copy-start(f32[4,4096]{1,0:T(4,128)} %get-tuple-element.76) | copy-start | bytes 196612
  280.3 14.8 %copy-start.16 = (f32[4,4096]{1,0:T(4,128)S(1)}, f32[4,4096]{1,0:T(4,128)}, u32[]{:S(2)}) copy-start(f32[4,4096]{1,0:T(4,128)} %get-tuple-element.77) | copy-start | bytes 196612
  280.3 15.3 %copy-start.10 = (f32[64,896]{1,0:T(8,128)S(1)}, f32[64,896]{1,0:T(8,128)}, u32[]{:S(2)}) copy-start(f32[64,896]{1,0:T(8,128)} %get-tuple-element.78) | copy-start | bytes 688132
  280.3 17.7 %copy-start.7 = (f32[64,896]{1,0:T(8,128)S(1)}, f32[64,896]{1,0:T(8,128)}, u32[]{:S(2)}) copy-start(f32[64,896]{1,0:T(8,128)} %get-tuple-element.53) | copy-start | bytes 688132
  280.3 17.7 %copy-start.8 = (f32[64,896]{1,0:T(8,128)S(1)}, f32[64,896]{1,0:T(8,128)}, u32[]{:S(2)}) copy-start(f32[64,896]{1,0:T(8,128)} %get-tuple-element.61) | copy-start | bytes 688132
  280.4 17.7 %copy-start.9 = (f32[64,896]{1,0:T(8,128)S(1)}, f32[64,896]{1,0:T(8,128)}, u32[]{:S(2)}) copy-start(f32[64,896]{1,0:T(8,128)} %get-tuple-element.74) | copy-start | bytes 688132
  296.6 6.7 %collective-permute-start.25 = (f32[2,2,8,1152]{3,2,1,0:T(8,128)S(1)}, f32[2,2,8,1152]{3,2,1,0:T(8,128)S(1)}, u32[]{:S(2)}, u32[]{:S(2)}) collective-permute-start(f32[2,2,8,1152]{3,2,1,0:T(8,128)S(1)} %fusion.3), channel_id=1, source_target_pairs={{0,4},{4,0},{8,12},{12,8},{16,20},{20,16},{24,28},{28,24},{1,5},{5... | collective-permute-start | bytes 442376 | tf_op jit(solution)/shard_map/ppermute | solution.py:16
  298.1 7.8 %collective-permute-start.23 = (f32[2,2,8,1152]{3,2,1,0:T(8,128)S(1)}, f32[2,2,8,1152]{3,2,1,0:T(8,128)S(1)}, u32[]{:S(2)}, u32[]{:S(2)}) collective-permute-start(f32[2,2,8,1152]{3,2,1,0:T(8,128)S(1)} %fusion.8), channel_id=1, source_target_pairs={{0,4},{4,0},{8,12},{12,8},{16,20},{20,16},{24,28},{28,24},{1,5},{5... | collective-permute-start | bytes 442376 | tf_op jit(solution)/shard_map/ppermute | solution.py:16
  303.4 8.1 %collective-permute-start.26 = (f32[2,8,1152]{2,1,0:T(8,128)S(1)}, f32[2,8,1152]{2,1,0:T(8,128)S(1)}, u32[]{:S(2)}, u32[]{:S(2)}) collective-permute-start(f32[2,8,1152]{2,1,0:T(8,128)S(1)} %dynamic-slice_bitcast_fusion.1), channel_id=1, source_target_pairs={{0,16},{4,20},{8,24},{12,28},{16,0},{20,4},{24,8},{28,12},{1,17},{... | collective-permute-start | bytes 221192 | tf_op jit(solution)/shard_map/ppermute | solution.py:16
  306.0 6.8 %collective-permute-start.24 = (f32[2,8,1152]{2,1,0:T(8,128)S(1)}, f32[2,8,1152]{2,1,0:T(8,128)S(1)}, u32[]{:S(2)}, u32[]{:S(2)}) collective-permute-start(f32[2,8,1152]{2,1,0:T(8,128)S(1)} %dynamic-slice_bitcast_fusion.2), channel_id=1, source_target_pairs={{0,16},{4,20},{8,24},{12,28},{16,0},{20,4},{24,8},{28,12},{1,17},{... | collective-permute-start | bytes 221192 | tf_op jit(solution)/shard_map/ppermute | solution.py:16
  314.0 7.8 %collective-permute-start.27 = (f32[8,1792]{1,0:T(8,128)S(1)}, f32[8,1792]{1,0:T(8,128)S(1)}, u32[]{:S(2)}, u32[]{:S(2)}) collective-permute-start(f32[8,1792]{1,0:T(8,128)S(1)} %fusion.13), channel_id=1, source_target_pairs={{0,8},{4,12},{8,0},{12,4},{16,24},{20,28},{24,16},{28,20},{1,9},{5... | collective-permute-start | bytes 172040 | tf_op jit(solution)/shard_map/ppermute | solution.py:16
  318.5 11.7 %all-to-all-start.1 = ((f32[32,1,1152]{2,1,0:T(1,128)}), f32[32,1,1152]{2,1,0:T(1,128)S(1)}, u32[]{:S(2)}, u32[]{:S(2)}) async-start(f32[32,1,1152]{2,1,0:T(1,128)} %all_to_all.25), calls=%async_computation.1 | async-start | bytes 294912 | tf_op jit(solution)/shard_map/all_to_all | solution.py:424
where the time goes:
time: 343 us; the launch traced here: 338 us
  waiting for transfers between devices  110 us (32%)
  Pallas kernels  104 us (30%)
  starting transfers between devices  36.3 us (11%)
  local copies, waits for them, and re-layouts  35.3 us (10%)
  matrix products  22.8 us (7%)
  other arithmetic  18.9 us (6%)
  between operations  10.6 us (3%)
    pallas_call x6, Pallas kernels, products(): pl.pallas_call(functools.partial(products_kernel, spans, parts, resumed,...  104 us
    ppermute x28, waiting for transfers between devices, swap(): return lax.ppermute(value, axis, [(a, a ^ stride) for a in range(size)])  102 us
    ppermute x28, starting transfers between devices, swap(): return lax.ppermute(value, axis, [(a, a ^ stride) for a in range(size)])  29.7 us
    dot_general x5, matrix products, mix_of(): jnp.dot(rows, left_diag, preferred_element_type=jnp.float32)  22.8 us
    mul x1, local copies, waits for them, and re-layouts, local(): left_rows[:, :, :, None] * eye_left[:, None, None, :]  11.8 us
    all_to_all x1, waiting for transfers between devices, local(): lax.all_to_all(outgoing.reshape((-1,) + outgoing.shape[2:]), ('dp', 'tens...  8.38 us
    mul x1, other arithmetic, local(): left_rows[:, :, :, None] * eye_left[:, None, None, :]  7.07 us
  transfers between devices with their start and end apart: 30, of which 14 were waited for; matrix products, arithmetic and copies ran while one was open for 16% of the time, Pallas kernels for 24%

commit v1 on v0

--- a/solution.py
+++ b/solution.py
@@ -62,7 +62,7 @@
     depth = piece_buf.shape[0] // count
     slots = rows_buf.shape[1] // depth
     offsets = [sum(spans[:which]) for which in range(len(spans))]
-    early = count - 2 if resumed else 0
+    early = count - 2 if 0 < resumed < tokens else 0
 
     def start_of(slot):
         return pl.multiple_of(starts_ref[slot] * depth, depth)
@@ -126,13 +126,9 @@
         def go_on(at):
             total[at] = total[at] - contract(rows_buf[at, here], piece_buf[here], 1, 0)
 
-        if low < early:
-            each_tile(resumed, tokens, go_on if low else start_rows)
-        elif low:
+        if low >= early:
             each_tile(0, resumed, go_on)
-            each_tile(resumed, tokens, go_on)
-        else:
-            each_tile(0, tokens, start_rows)
+        each_tile(resumed, tokens, go_on if low else start_rows)
     if not finish:
         return
 
@@ -193,7 +189,7 @@
         pltpu.VMEM((count * depth, columns), jnp.bfloat16),
         pltpu.SemaphoreType.DMA(((slots + 1) * len(spans) + 1 + sum(parts),)),
     ]
-    flops = 2 * columns * depth * (tokens * count - resumed * (count - 2))
+    flops = 2 * columns * depth * tokens * count
     if finish:
         shapes = [(mid_columns // blocks, columns), (blocks, features), (1, columns)]
         scratch = [pltpu.VMEM((tokens, columns), jnp.float32)] + scratch
@@ -341,8 +337,11 @@
         mine[0] = after(mine[0], waits)
         pieces = [halves.get((chunk, mask), [held[chunk].get(mask)]) for mask in order[:end]]
         finish = end == len(order)
+        places = starts[:end]
+        if partial is not None:
+            pieces, places = pieces[-2:], jnp.concatenate([starts[-2:], starts[:-2]])
         terms = products(
-            [token_sets[item] for item in which], mine, right_diags[chunk], pieces, starts[:end], chunk_blocks,
+            [token_sets[item] for item in which], mine, right_diags[chunk], pieces, places, chunk_blocks,
             1.0 / total_tokens, partial=partial, finish=finish,
         )
         if not finish:
@@ -350,6 +349,23 @@
             return terms
         previous = terms[2]
         sums[chunk].append(terms)
+
+    def gather_rows(terms):
+        right_sum, left_sum = sum(term[0] for term in terms), sum(term[1] for term in terms)
+        left_sum = left_sum.reshape(chunk_blocks, mids, in_size).transpose(2, 0, 1).reshape(in_size, chunk_blocks * mids)
+        both = jnp.concatenate([right_sum, left_sum], 1)
+        return both.reshape((2,) * bits + (both.shape[0] // dp_count, both.shape[1]))
+
+    def sum_by_halving(both):
+        places = [s for s in reversed(strides)]
+        for stride in [near, far] + strides[:grouped]:
+            at = places.index(stride)
+            bit = (dp_pos // stride) % 2
+            away = lax.dynamic_index_in_dim(both, 1 - bit, at, keepdims=False)
+            kept = lax.dynamic_index_in_dim(both, bit, at, keepdims=False)
+            both = kept + swap(away, "dp", stride)
+            places.remove(stride)
+        return both
 
     if last:
         source, cut = held[last][pair], unit_rows // 2
@@ -375,29 +391,17 @@
         mixes[late[0]] = mix_of(token_sets[late[0]], left_diag)
         run([0, *early], last, partial=partial, waits=[mixes[late[0]]])
         run(late, 0)
-        run(late, last)
+        first_rows = gather_rows(sums[0])
+        summed = [sum_by_halving(first_rows)]
+        run(late, last, waits=[first_rows])
     else:
         for which in range(3):
             token_sets += share_tokens(fetch_tokens(which, early_done))
         run(range(len(token_sets)), 0)
-
-    loss_part = 0.0
-    summed = []
-    for terms in sums:
-        right_sum, left_sum = sum(term[0] for term in terms), sum(term[1] for term in terms)
-        loss_part = loss_part + sum(jnp.sum(term[2]) for term in terms)
-        left_sum = left_sum.reshape(chunk_blocks, mids, in_size).transpose(2, 0, 1).reshape(in_size, chunk_blocks * mids)
-        both = jnp.concatenate([right_sum, left_sum], 1)
-        both = both.reshape((2,) * bits + (both.shape[0] // dp_count, both.shape[1]))
-        places = [s for s in reversed(strides)]
-        for stride in [near, far] + strides[:grouped]:
-            at = places.index(stride)
-            bit = (dp_pos // stride) % 2
-            away = lax.dynamic_index_in_dim(both, 1 - bit, at, keepdims=False)
-            kept = lax.dynamic_index_in_dim(both, bit, at, keepdims=False)
-            both = kept + swap(away, "dp", stride)
-            places.remove(stride)
-        summed.append(both)
+        summed = []
+    summed.append(sum_by_halving(gather_rows(sums[last])))
+    loss_part = sum(jnp.sum(term[2]) for terms in sums for term in terms)
+
     right_both = jnp.concatenate([both[..., :chunk_columns] for both in summed], -1)
     left_both = jnp.concatenate([both[..., chunk_columns:] for both in summed], -1)
 

time: 343 us -> 339 us (0.988)
  Pallas kernels: 104 us -> 99.6 us
    pallas_call x6, Pallas kernels: 104 us -> 99.6 us  [products(): pl.pallas_call(functools.partial(products_kernel, spans, parts, resumed,...]
  transfers between devices with their start and end apart: 30 -> 30, of which waited for: 14 -> 15; matrix products, arithmetic and copies ran while one was open for 16% -> 16% of each run, Pallas kernels for 24% -> 22%
where the time goes in v1:
time: 339 us; the launch traced here: 335 us
  waiting for transfers between devices  109 us (32%)
  Pallas kernels  99.6 us (29%)
  starting transfers between devices  37.2 us (11%)
  local copies, waits for them, and re-layouts  36.3 us (11%)
  matrix products  22.8 us (7%)
  other arithmetic  18.9 us (6%)
  between operations  10.5 us (3%)
    ppermute x28, waiting for transfers between devices, swap(): return lax.ppermute(value, axis, [(a, a ^ stride) for a in range(size)])  101 us
    pallas_call x6, Pallas kernels, products(): pl.pallas_call(functools.partial(products_kernel, spans, parts, resumed,...  99.6 us
    ppermute x28, starting transfers between devices, swap(): return lax.ppermute(value, axis, [(a, a ^ stride) for a in range(size)])  31.1 us
    dot_general x5, matrix products, mix_of(): jnp.dot(rows, left_diag, preferred_element_type=jnp.float32)  22.8 us
    mul x1, local copies, waits for them, and re-layouts, local(): left_rows[:, :, :, None] * eye_left[:, None, None, :]  11.8 us
    all_to_all x1, waiting for transfers between devices, local(): lax.all_to_all(outgoing.reshape((-1,) + outgoing.shape[2:]), ('dp', 'tens...  8.38 us
    mul x1, other arithmetic, local(): left_rows[:, :, :, None] * eye_left[:, None, None, :]  7.08 us
  transfers between devices with their start and end apart: 30, of which 15 were waited for; matrix products, arithmetic and copies ran while one was open for 16% of the time, Pallas kernels for 22%

profile of v1, /device:TPU:0, one launch (start us, length us, event | category | flops | bytes accessed | tf_op | source)
XLA Modules:
  0.0 334.7 jit_solution(4273713721791825640)
XLA Ops:
  0.7 3.7 %constant_dynamic-slice_fusion.5 = (bf16[512,896]{1,0:T(8,128)(2,1)}, bf16[512,896]{1,0:T(8,128)(2,1)}, bf16[512,896]{1,0:T(8,128)(2,1)S(1)}, bf16[512,896]{1,0:T(8,128)(2,1)S(1)}) fusion(bf16[512,3584]{1,0:T(8,128)(2,1)} %param.5, s32[]{:T(128)S(6)} %select_n.147, s32[]{:T(128)S(6)} %select_n.143, s32[]{:T(128)S(6)} %select_n.141, s32[]{:T(128)S(6)} %select_n.144), kind=kLoop, calls=%fused_computation.73 | loop fusion | bytes 7340048 | tf_op jit(solution)/shard_map/dynamic_slice | solution.py:252
  4.4 3.0 collective-permute-start.1
  7.4 1.5 collective-permute-start.3
  9.5 2.6 collective-permute-start
  12.1 1.2 compare_select_fusion.1
  13.9 1.2 constant_dynamic-slice_fusion.6
  15.1 31.2 %collective-permute-done.1.refs_4_.refs_6_ = bf16[512,896]{1,0:T(8,128)(2,1)} collective-permute-done((bf16[512,896]{1,0:T(8,128)(2,1)}, bf16[512,896]{1,0:T(8,128)(2,1)}, u32[]{:S(2)}, u32[]{:S(2)}) %collective-permute-start.1) | collective-permute-done | bytes 917536 | tf_op jit(solution)/shard_map/ppermute | solution.py:16
  46.4 2.6 collective-permute-done.2.refs_3_.refs_5_
  49.0 2.4 collective-permute-done.refs_5_.refs_7_
  52.0 0.9 reshape.123
  52.9 3.3 all-to-all-start
  56.2 1.6 collective-permute-start.5
  58.5 2.9 collective-permute-start.7
  62.2 7.1 %broadcast_multiply_fusion = bf16[64,64,8,64]{3,2,1,0:T(8,128)(2,1)} fusion(bf16[64,64]{1,0:T(8,128)(2,1)S(1)} %fusion.16, bf16[64,64,8]{2,1,0:T(8,128)(2,1)S(1)} %copy.35), kind=kLoop, calls=%fused_computation | loop fusion | flops 2097152 | bytes 4268032 | tf_op jit(solution)/shard_map/mul | solution.py:304
  69.2 11.8 %mul.65 = bf16[4096,512]{1,0:T(8,128)(2,1)} reshape(bf16[64,64,8,64]{3,2,1,0:T(8,128)(2,1)} %broadcast_multiply_fusion) | data formatting | bytes 8388608 | tf_op jit(solution)/shard_map/mul | solution.py:304
  81.1 8.7 %fusion = bf16[960,512]{1,0:T(8,128)(2,1)S(1)} fusion(bf16[960,4096]{1,0:T(8,128)(2,1)} %refs_0_.5, bf16[4096,512]{1,0:T(8,128)(2,1)} %mul.65), kind=kOutput, calls=%fused_computation.2 | convolution fusion | flops 4027023360 | bytes 13041664 | tf_op jit(solution)/shard_map/dot_general | solution.py:219
  89.8 11.3 %collective-permute-done.4.refs_8_.refs_10_ = bf16[512,896]{1,0:T(8,128)(2,1)} collective-permute-done((bf16[512,896]{1,0:T(8,128)(2,1)}, bf16[512,896]{1,0:T(8,128)(2,1)}, u32[]{:S(2)}, u32[]{:S(2)}) %collective-permute-start.4) | collective-permute-done | bytes 917536 | tf_op jit(solution)/shard_map/ppermute | solution.py:16
  101.4 1.4 collective-permute-start.9
  102.8 2.1 collective-permute-start.10
  105.4 1.3 constant_dynamic-slice_fusion.3
  106.7 1.0 fusion.20
  107.8 0.8 fusion.21
  108.6 32.8 %collective-permute-done.8 = bf16[112,4096]{1,0:T(8,128)(2,1)S(1)} collective-permute-done((bf16[112,4096]{1,0:T(8,128)(2,1)S(1)}, bf16[112,4096]{1,0:T(8,128)(2,1)S(1)}, u32[]{:S(2)}, u32[]{:S(2)}) %collective-permute-start.8) | collective-permute-done | bytes 917536 | tf_op jit(solution)/shard_map/ppermute | solution.py:16
  141.4 3.0 collective-permute-done.10.refs_9_.refs_7_
  145.4 1.2 collective-permute-start.14
  146.6 1.4 collective-permute-start.12
  148.0 2.1 collective-permute-start.15
  150.1 19.2 %shard_map.67 = (f32[64,896]{1,0:T(8,128)}, f32[4,4096]{1,0:T(4,128)}, f32[1,896]{1,0:T(1,128)}) custom-call(s32[8]{0:T(128)} %stack.54.starts_ref, bf16[256,896]{1,0:T(8,128)(2,1)} %get-tuple-element.119.right_ref, bf16[960,4096]{1,0:T(8,128)(2,1)} %refs_0_.5, bf16[960,256]{1,0:T(8,128)(2,1)} %get-tuple-element.52.refs_1_, bf16[512,896]{1,0:T(8,128)(2,1)} %copy-done.4, ...), custom_call_target="tpu_custom_call" | custom-call | flops 9940500480 | bytes 15204352 | tf_op jit(solution)/shard_map/pallas_call | solution.py:204
  169.3 1.0 constant_dynamic-update-slice_fusion.1
  170.3 1.1 constant_dynamic-update-slice_fusion.refs_0_.refs_1_
  172.0 0.9 collective-permute-start.18
  172.9 1.5 collective-permute-start.17
  174.5 4.0 %convolution_convert_fusion.4 = bf16[224,512]{1,0:T(8,128)(2,1)S(1)} fusion(bf16[224,4096]{1,0:T(8,128)(2,1)} %constant_dynamic-update-slice_fusion.refs_0_.refs_1_, bf16[4096,512]{1,0:T(8,128)(2,1)} %mul.65), kind=kOutput, calls=%fused_computation.6 | convolution fusion | flops 939638784 | bytes 6258688 | tf_op jit(solution)/shard_map/dot_general | solution.py:219
  179.2 2.6 convolution_convert_fusion.3
  182.6 11.5 %shard_map.68 = (f32[64,896]{1,0:T(8,128)}, f32[4,4096]{1,0:T(4,128)}, f32[1,896]{1,0:T(1,128)}) custom-call(s32[8]{0:T(128)} %stack.54.starts_ref, bf16[256,896]{1,0:T(8,128)(2,1)} %get-tuple-element.119.right_ref, bf16[224,4096]{1,0:T(8,128)(2,1)} %constant_dynamic-update-slice_fusion.refs_0_.refs_1_, ...), custom_call_target="tpu_custom_call" | custom-call | flops 4638900224 | bytes 11010048 | tf_op jit(solution)/shard_map/pallas_call | solution.py:204
  194.1 1.5 collective-permute-done.18.refs_7_.refs_11_
  195.7 1.2 collective-permute-done.17
  197.2 1.8 collective-permute-start.21
  199.1 17.8 %shard_map.69.refs_10_ = f32[1408,896]{1,0:T(8,128)} custom-call(s32[6]{0:T(128)} %stack.55.starts_ref, bf16[256,896]{1,0:T(8,128)(2,1)} %get-tuple-element.120.right_ref, bf16[960,4096]{1,0:T(8,128)(2,1)} %refs_0_.5, bf16[224,4096]{1,0:T(8,128)(2,1)} %constant_dynamic-update-slice_fusion.refs_0_.refs_1_, ...), custom_call_target="tpu_custom_call" | custom-call | flops 7751073792 | bytes 14155776 | tf_op jit(solution)/shard_map/pallas_call | solution.py:204
  217.0 1.8 collective-permute-done.21.refs_9_.refs_13_
  218.9 4.1 %collective-permute-done.19 = bf16[128,4096]{1,0:T(8,128)(2,1)S(1)} collective-permute-done((bf16[128,4096]{1,0:T(8,128)(2,1)S(1)}, bf16[128,4096]{1,0:T(8,128)(2,1)S(1)}, u32[]{:S(2)}, u32[]{:S(2)}) %collective-permute-start.19) | collective-permute-done | bytes 1048608 | tf_op jit(solution)/shard_map/ppermute | solution.py:16
  223.2 0.8 concatenate.48.starts_ref
  226.8 3.4 %convolution_convert_fusion.2 = bf16[256,512]{1,0:T(8,128)(2,1)S(1)} fusion(bf16[256,4096]{1,0:T(8,128)(2,1)S(1)} %constant_dynamic-update-slice_fusion.4.refs_0_, bf16[4096,512]{1,0:T(8,128)(2,1)} %mul.65), kind=kOutput, calls=%fused_computation.4 | convolution fusion | flops 1073872896 | bytes 6553600 | tf_op jit(solution)/shard_map/dot_general | solution.py:219
  230.2 26.8 %shard_map.70 = (f32[64,896]{1,0:T(8,128)}, f32[4,4096]{1,0:T(4,128)}, f32[1,896]{1,0:T(1,128)}) custom-call(s32[8]{0:T(128)} %concatenate.48.starts_ref, bf16[256,896]{1,0:T(8,128)(2,1)} %get-tuple-element.120.right_ref, bf16[960,4096]{1,0:T(8,128)(2,1)} %refs_0_.5, bf16[224,4096]{1,0:T(8,128)(2,1)} %constant_dynamic-update-slice_fusion.refs_0_.refs_1_, ...), custom_call_target="tpu_custom_call" | custom-call | flops 6828326912 | bytes 13369344 | tf_op jit(solution)/shard_map/pallas_call | solution.py:204
  257.0 1.3 reduce_sum.97
  258.3 0.7 fusion.24
  259.1 4.1 %convolution_convert_fusion.1 = bf16[256,512]{1,0:T(8,128)(2,1)S(1)} fusion(bf16[256,4096]{1,0:T(8,128)(2,1)} %collective-permute-done.22.refs_1_, bf16[4096,512]{1,0:T(8,128)(2,1)} %mul.65), kind=kOutput, calls=%fused_computation.3 | convolution fusion | flops 1073872896 | bytes 6553600 | tf_op jit(solution)/shard_map/dot_general | solution.py:219
  263.9 12.1 %shard_map.71 = (f32[64,896]{1,0:T(8,128)}, f32[4,4096]{1,0:T(4,128)}, f32[1,896]{1,0:T(1,128)}) custom-call(s32[8]{0:T(128)} %stack.54.starts_ref, bf16[256,896]{1,0:T(8,128)(2,1)} %get-tuple-element.119.right_ref, bf16[256,4096]{1,0:T(8,128)(2,1)} %copy-done.5, bf16[256,4096]{1,0:T(8,128)(2,1)} %collective-permute-done.22.refs_1_, ...), custom_call_target="tpu_custom_call" | custom-call | flops 5301600256 | bytes 11534336 | tf_op jit(solution)/shard_map/pallas_call | solution.py:204
  276.0 1.3 reduce_sum.96
  277.3 12.2 %shard_map.72 = (f32[64,896]{1,0:T(8,128)}, f32[4,4096]{1,0:T(4,128)}, f32[1,896]{1,0:T(1,128)}) custom-call(s32[8]{0:T(128)} %stack.54.starts_ref, bf16[256,896]{1,0:T(8,128)(2,1)} %get-tuple-element.120.right_ref, bf16[256,4096]{1,0:T(8,128)(2,1)} %copy-done.5, bf16[256,4096]{1,0:T(8,128)(2,1)} %collective-permute-done.22.refs_1_, ...), custom_call_target="tpu_custom_call" | custom-call | flops 5301600256 | bytes 11534336 | tf_op jit(solution)/shard_map/pallas_call | solution.py:204
  289.5 1.4 reduce_sum.98
  290.9 0.9 add.192
  292.6 1.0 add.191
  294.1 1.7 collective-permute-start.23
  297.7 2.6 collective-permute-done.25
  300.4 1.1 collective-permute-start.26
  301.4 1.4 collective-permute-done.23
  302.9 1.1 collective-permute-start.24
  303.9 4.8 %collective-permute-done.26 = f32[2,8,1152]{2,1,0:T(8,128)S(1)} collective-permute-done((f32[2,8,1152]{2,1,0:T(8,128)S(1)}, f32[2,8,1152]{2,1,0:T(8,128)S(1)}, u32[]{:S(2)}, u32[]{:S(2)}) %collective-permute-start.26) | collective-permute-done | bytes 73760 | tf_op jit(solution)/shard_map/ppermute | solution.py:16
  315.0 0.8 all_to_all.25
  315.8 2.8 all-to-all-start.1
  318.7 8.4 %all-to-all-done.1 = f32[32,1,1152]{2,1,0:T(1,128)S(1)} async-done(((f32[32,1,1152]{2,1,0:T(1,128)}), f32[32,1,1152]{2,1,0:T(1,128)S(1)}, u32[]{:S(2)}, u32[]{:S(2)}) %all-to-all-start.1) | async-done | bytes 147488 | tf_op jit(solution)/shard_map/all_to_all | solution.py:428
  329.1 1.1 reshape.121
  330.7 1.4 mul.71
  (152 shorter events, 17.1 us)
Async XLA Ops:
  0.7 11.4 %copy-start.12 = (bf16[64,3584]{1,0:T(8,128)(2,1)S(1)}, bf16[64,3584]{1,0:T(8,128)(2,1)}, u32[]{:S(2)}) copy-start(bf16[64,3584]{1,0:T(8,128)(2,1)} %param.7) | copy-start | bytes 1376260
  0.7 50.7 %copy-start.11 = (bf16[64,1024]{1,0:T(8,128)(2,1)S(1)}, bf16[64,1024]{1,0:T(8,128)(2,1)}, u32[]{:S(2)}) copy-start(bf16[64,1024]{1,0:T(8,128)(2,1)} %param.6) | copy-start | bytes 393220
  4.4 44.6 %copy-start.2 = (bf16[512,896]{1,0:T(8,128)(2,1)}, bf16[512,896]{1,0:T(8,128)(2,1)S(1)}, u32[]{:S(2)}) copy-start(bf16[512,896]{1,0:T(8,128)(2,1)S(1)} %get-tuple-element.50.refs_6_.refs_4_) | copy-start | bytes 2752516
  4.4 53.6 %copy-start.4 = (bf16[512,896]{1,0:T(8,128)(2,1)}, bf16[512,896]{1,0:T(8,128)(2,1)S(1)}, u32[]{:S(2)}) copy-start(bf16[512,896]{1,0:T(8,128)(2,1)S(1)} %get-tuple-element.89.refs_2_.refs_4_) | copy-start | bytes 2752516
  4.4 42.0 %collective-permute-start.1 = (bf16[512,896]{1,0:T(8,128)(2,1)}, bf16[512,896]{1,0:T(8,128)(2,1)}, u32[]{:S(2)}, u32[]{:S(2)}) collective-permute-start(bf16[512,896]{1,0:T(8,128)(2,1)} %get-tuple-element.88), channel_id=1, source_target_pairs={{0,8},{4,12},{8,0},{12,4},{16,24},{20,28},{24,16},{28,20},{1,9},{5... | collective-permute-start | bytes 2752520 | tf_op jit(solution)/shard_map/ppermute | solution.py:16
  7.4 39.0 %collective-permute-start.3 = (bf16[512,896]{1,0:T(8,128)(2,1)S(1)}, bf16[512,896]{1,0:T(8,128)(2,1)}, u32[]{:S(2)}, u32[]{:S(2)}) collective-permute-start(bf16[512,896]{1,0:T(8,128)(2,1)S(1)} %get-tuple-element.50.refs_6_.refs_4_), channel_id=1, source_target_pairs={{0,4},{4,0},{8,12},{12,8},{16,20},{20,16},{24,28},{28,24},{1,5},{5... | collective-permute-start | bytes 2752520 | tf_op jit(solution)/shard_map/ppermute | solution.py:16
  8.9 40.1 %collective-permute-start.2 = (bf16[512,896]{1,0:T(8,128)(2,1)S(1)}, bf16[512,896]{1,0:T(8,128)(2,1)}, u32[]{:S(2)}, u32[]{:S(2)}) collective-permute-start(bf16[512,896]{1,0:T(8,128)(2,1)S(1)} %get-tuple-element.89.refs_2_.refs_4_), channel_id=1, source_target_pairs={{0,4},{4,0},{8,12},{12,8},{16,20},{20,16},{24,28},{28,24},{1,5},{5... | collective-permute-start | bytes 2752520 | tf_op jit(solution)/shard_map/ppermute | solution.py:16
  9.5 42.0 %collective-permute-start = (bf16[512,896]{1,0:T(8,128)(2,1)S(1)}, bf16[512,896]{1,0:T(8,128)(2,1)}, u32[]{:S(2)}, u32[]{:S(2)}) collective-permute-start(bf16[512,896]{1,0:T(8,128)(2,1)S(1)} %get-tuple-element.89.refs_2_.refs_4_), channel_id=1, source_target_pairs={{0,16},{4,20},{8,24},{12,28},{16,0},{20,4},{24,8},{28,12},{1,17},{... | collective-permute-start | bytes 2752520 | tf_op jit(solution)/shard_map/ppermute | solution.py:16
  52.9 8.5 %all-to-all-start = ((bf16[4,2,8192]{2,1,0:T(2,128)(2,1)}), bf16[4,2,8192]{2,1,0:T(2,128)(2,1)S(1)}, u32[]{:S(2)}, u32[]{:S(2)}) async-start(bf16[4,2,8192]{2,1,0:T(2,128)(2,1)} %reshape.123), calls=%async_computation | async-start | bytes 262144 | tf_op jit(solution)/shard_map/all_to_all | solution.py:300
  56.2 33.5 %collective-permute-start.5 = (bf16[512,896]{1,0:T(8,128)(2,1)}, bf16[512,896]{1,0:T(8,128)(2,1)}, u32[]{:S(2)}, u32[]{:S(2)}) collective-permute-start(bf16[512,896]{1,0:T(8,128)(2,1)} %collective-permute-done.1.refs_4_.refs_6_), channel_id=1, source_target_pairs={{0,4},{4,0},{8,12},{12,8},{16,20},{20,16},{24,28},{28,24},{1,5},{5... | collective-permute-start | bytes 2752520 | tf_op jit(solution)/shard_map/ppermute | solution.py:16
  57.8 43.3 %collective-permute-start.4 = (bf16[512,896]{1,0:T(8,128)(2,1)}, bf16[512,896]{1,0:T(8,128)(2,1)}, u32[]{:S(2)}, u32[]{:S(2)}) collective-permute-start(bf16[512,896]{1,0:T(8,128)(2,1)} %collective-permute-done.1.refs_4_.refs_6_), channel_id=1, source_target_pairs={{0,16},{4,20},{8,24},{12,28},{16,0},{20,4},{24,8},{28,12},{1,17},{... | collective-permute-start | bytes 2752520 | tf_op jit(solution)/shard_map/ppermute | solution.py:16
  58.0 43.1 %collective-permute-start.6 = (bf16[512,896]{1,0:T(8,128)(2,1)}, bf16[512,896]{1,0:T(8,128)(2,1)}, u32[]{:S(2)}, u32[]{:S(2)}) collective-permute-start(bf16[512,896]{1,0:T(8,128)(2,1)} %collective-permute-done.refs_5_.refs_7_), channel_id=1, source_target_pairs={{0,4},{4,0},{8,12},{12,8},{16,20},{20,16},{24,28},{28,24},{1,5},{5... | collective-permute-start | bytes 2752520 | tf_op jit(solution)/shard_map/ppermute | solution.py:16
  58.5 42.8 %collective-permute-start.7 = (bf16[512,896]{1,0:T(8,128)(2,1)}, bf16[512,896]{1,0:T(8,128)(2,1)S(1)}, u32[]{:S(2)}, u32[]{:S(2)}) collective-permute-start(bf16[512,896]{1,0:T(8,128)(2,1)} %get-tuple-element.47), channel_id=1, source_target_pairs={{0,8},{4,12},{8,0},{12,4},{16,24},{20,28},{24,16},{28,20},{1,9},{5... | collective-permute-start | bytes 2752520 | tf_op jit(solution)/shard_map/ppermute | solution.py:16
  81.1 21.7 %copy-start.3 = (bf16[512,896]{1,0:T(8,128)(2,1)S(1)}, bf16[512,896]{1,0:T(8,128)(2,1)}, u32[]{:S(2)}) copy-start(bf16[512,896]{1,0:T(8,128)(2,1)} %copy-done.2) | copy-start | bytes 2752516
  101.3 67.9 %copy-start.1 = (bf16[512,896]{1,0:T(8,128)(2,1)}, bf16[512,896]{1,0:T(8,128)(2,1)S(1)}, u32[]{:S(2)}) copy-start(bf16[512,896]{1,0:T(8,128)(2,1)S(1)} %collective-permute-done.7.refs_8_.refs_6_) | copy-start | bytes 2752516
  101.3 40.1 %collective-permute-start.8 = (bf16[112,4096]{1,0:T(8,128)(2,1)S(1)}, bf16[112,4096]{1,0:T(8,128)(2,1)S(1)}, u32[]{:S(2)}, u32[]{:S(2)}) collective-permute-start(bf16[112,4096]{1,0:T(8,128)(2,1)S(1)} %constant_dynamic-slice_fusion.6), channel_id=1, source_target_pairs={{0,8},{4,12},{8,0},{12,4},{16,24},{20,28},{24,16},{28,20},{1,9},{5... | collective-permute-start | bytes 2752520 | tf_op jit(solution)/shard_map/ppermute | solution.py:16
  101.4 40.1 %collective-permute-start.9 = (bf16[512,896]{1,0:T(8,128)(2,1)}, bf16[512,896]{1,0:T(8,128)(2,1)S(1)}, u32[]{:S(2)}, u32[]{:S(2)}) collective-permute-start(bf16[512,896]{1,0:T(8,128)(2,1)} %collective-permute-done.4.refs_8_.refs_10_), channel_id=1, source_target_pairs={{0,4},{4,0},{8,12},{12,8},{16,20},{20,16},{24,28},{28,24},{1,5},{5... | collective-permute-start | bytes 2752520 | tf_op jit(solution)/shard_map/ppermute | solution.py:16
  102.8 41.6 %collective-permute-start.10 = (bf16[512,896]{1,0:T(8,128)(2,1)S(1)}, bf16[512,896]{1,0:T(8,128)(2,1)S(1)}, u32[]{:S(2)}, u32[]{:S(2)}) collective-permute-start(bf16[512,896]{1,0:T(8,128)(2,1)S(1)} %copy-done.3), channel_id=1, source_target_pairs={{0,16},{4,20},{8,24},{12,28},{16,0},{20,4},{24,8},{28,12},{1,17},{... | collective-permute-start | bytes 2752520 | tf_op jit(solution)/shard_map/ppermute | solution.py:16
  104.9 39.5 %collective-permute-start.11 = (bf16[512,896]{1,0:T(8,128)(2,1)S(1)}, bf16[512,896]{1,0:T(8,128)(2,1)S(1)}, u32[]{:S(2)}, u32[]{:S(2)}) collective-permute-start(bf16[512,896]{1,0:T(8,128)(2,1)S(1)} %collective-permute-done.7.refs_8_.refs_6_), channel_id=1, source_target_pairs={{0,4},{4,0},{8,12},{12,8},{16,20},{20,16},{24,28},{28,24},{1,5},{5... | collective-permute-start | bytes 2752520 | tf_op jit(solution)/shard_map/ppermute | solution.py:16
  141.4 8.6 %copy-start.21 = (bf16[512,896]{1,0:T(8,128)(2,1)}, bf16[512,896]{1,0:T(8,128)(2,1)S(1)}, u32[]{:S(2)}) copy-start(bf16[512,896]{1,0:T(8,128)(2,1)S(1)} %collective-permute-done.9.refs_9_.refs_11_) | copy-start | bytes 2752516
  144.4 24.9 %copy-start.19 = (bf16[512,896]{1,0:T(8,128)(2,1)}, bf16[512,896]{1,0:T(8,128)(2,1)S(1)}, u32[]{:S(2)}) copy-start(bf16[512,896]{1,0:T(8,128)(2,1)S(1)} %collective-permute-done.10.refs_9_.refs_7_) | copy-start | bytes 2752516
  144.4 1.0 copy-start.20
  144.4 25.9 %collective-permute-start.13 = (bf16[256,896]{1,0:T(8,128)(2,1)S(1)}, bf16[256,896]{1,0:T(8,128)(2,1)}, u32[]{:S(2)}, u32[]{:S(2)}) collective-permute-start(bf16[256,896]{1,0:T(8,128)(2,1)S(1)} %get-tuple-element.56), channel_id=1, source_target_pairs={{0,16},{4,20},{8,24},{12,28},{16,0},{20,4},{24,8},{28,12},{1,17},{... | collective-permute-start | bytes 1376264 | tf_op jit(solution)/shard_map/ppermute | solution.py:16
  145.4 24.9 %collective-permute-start.14 = (bf16[64,4096]{1,0:T(8,128)(2,1)S(1)}, bf16[64,4096]{1,0:T(8,128)(2,1)S(1)}, u32[]{:S(2)}, u32[]{:S(2)}) collective-permute-start(bf16[64,4096]{1,0:T(8,128)(2,1)S(1)} %get-tuple-element.57), channel_id=1, source_target_pairs={{0,8},{4,12},{8,0},{12,4},{16,24},{20,28},{24,16},{28,20},{1,9},{5... | collective-permute-start | bytes 1572872 | tf_op jit(solution)/shard_map/ppermute | solution.py:16
  146.6 23.6 %collective-permute-start.12 = (bf16[112,4096]{1,0:T(8,128)(2,1)S(1)}, bf16[112,4096]{1,0:T(8,128)(2,1)S(1)}, u32[]{:S(2)}, u32[]{:S(2)}) collective-permute-start(bf16[112,4096]{1,0:T(8,128)(2,1)S(1)} %collective-permute-done.8), channel_id=1, source_target_pairs={{0,2},{1,3},{2,0},{3,1},{4,6},{5,7},{6,4},{7,5},{8,10},{9,11},{10,... | collective-permute-start | bytes 2752520 | tf_op jit(solution)/shard_map/ppermute | solution.py:16
  148.0 22.3 %collective-permute-start.15 = (bf16[512,896]{1,0:T(8,128)(2,1)S(1)}, bf16[512,896]{1,0:T(8,128)(2,1)S(1)}, u32[]{:S(2)}, u32[]{:S(2)}) collective-permute-start(bf16[512,896]{1,0:T(8,128)(2,1)S(1)} %collective-permute-done.10.refs_9_.refs_7_), channel_id=1, source_target_pairs={{0,4},{4,0},{8,12},{12,8},{16,20},{20,16},{24,28},{28,24},{1,5},{5... | collective-permute-start | bytes 2752520 | tf_op jit(solution)/shard_map/ppermute | solution.py:16
  169.3 2.7 copy-start.6
  170.3 8.2 %copy-start.22 = (bf16[512,896]{1,0:T(8,128)(2,1)}, bf16[512,896]{1,0:T(8,128)(2,1)S(1)}, u32[]{:S(2)}) copy-start(bf16[512,896]{1,0:T(8,128)(2,1)S(1)} %collective-permute-done.15.refs_10_.refs_8_) | copy-start | bytes 2752516
  171.4 7.8 %collective-permute-start.16 = (bf16[224,4096]{1,0:T(8,128)(2,1)}, bf16[224,4096]{1,0:T(8,128)(2,1)}, u32[]{:S(2)}, u32[]{:S(2)}) collective-permute-start(bf16[224,4096]{1,0:T(8,128)(2,1)} %constant_dynamic-update-slice_fusion.refs_0_.refs_1_), channel_id=1, source_target_pairs={{0,1},{1,0},{2,3},{3,2},{4,5},{5,4},{6,7},{7,6},{8,9},{9,8},{10,11... | collective-permute-start | bytes 5505032 | tf_op jit(solution)/shard_map/ppermute | solution.py:16
  172.0 23.6 %collective-permute-start.18 = (bf16[256,896]{1,0:T(8,128)(2,1)S(1)}, bf16[256,896]{1,0:T(8,128)(2,1)S(1)}, u32[]{:S(2)}, u32[]{:S(2)}) collective-permute-start(bf16[256,896]{1,0:T(8,128)(2,1)S(1)} %copy-done.6), channel_id=1, source_target_pairs={{0,16},{4,20},{8,24},{12,28},{16,0},{20,4},{24,8},{28,12},{1,17},{... | collective-permute-start | bytes 1376264 | tf_op jit(solution)/shard_map/ppermute | solution.py:16
  172.9 23.9 %collective-permute-start.17 = (bf16[64,4096]{1,0:T(8,128)(2,1)S(1)}, bf16[64,4096]{1,0:T(8,128)(2,1)S(1)}, u32[]{:S(2)}, u32[]{:S(2)}) collective-permute-start(bf16[64,4096]{1,0:T(8,128)(2,1)S(1)} %get-tuple-element.62), channel_id=1, source_target_pairs={{0,8},{4,12},{8,0},{12,4},{16,24},{20,28},{24,16},{28,20},{1,9},{5... | collective-permute-start | bytes 1572872 | tf_op jit(solution)/shard_map/ppermute | solution.py:16
  174.5 4.7 %copy-start = (bf16[4096,512]{1,0:T(8,128)(2,1)S(1)}, bf16[4096,512]{1,0:T(8,128)(2,1)}, u32[]{:S(2)}) copy-start(bf16[4096,512]{1,0:T(8,128)(2,1)} %mul.65) | copy-start | bytes 12582916
  195.7 21.2 %copy-start.23 = (bf16[256,896]{1,0:T(8,128)(2,1)}, bf16[256,896]{1,0:T(8,128)(2,1)S(1)}, u32[]{:S(2)}) copy-start(bf16[256,896]{1,0:T(8,128)(2,1)S(1)} %collective-permute-done.18.refs_7_.refs_11_) | copy-start | bytes 1376260
  196.9 20.1 %collective-permute-start.20 = (bf16[256,896]{1,0:T(8,128)(2,1)}, bf16[256,896]{1,0:T(8,128)(2,1)S(1)}, u32[]{:S(2)}, u32[]{:S(2)}) collective-permute-start(bf16[256,896]{1,0:T(8,128)(2,1)} %collective-permute-done.13.refs_6_.refs_10_), channel_id=1, source_target_pairs={{0,4},{4,0},{8,12},{12,8},{16,20},{20,16},{24,28},{28,24},{1,5},{5... | collective-permute-start | bytes 1376264 | tf_op jit(solution)/shard_map/ppermute | solution.py:16
  197.2 21.7 %collective-permute-start.21 = (bf16[256,896]{1,0:T(8,128)(2,1)S(1)}, bf16[256,896]{1,0:T(8,128)(2,1)S(1)}, u32[]{:S(2)}, u32[]{:S(2)}) collective-permute-start(bf16[256,896]{1,0:T(8,128)(2,1)S(1)} %collective-permute-done.18.refs_7_.refs_11_), channel_id=1, source_target_pairs={{0,4},{4,0},{8,12},{12,8},{16,20},{20,16},{24,28},{28,24},{1,5},{5... | collective-permute-start | bytes 1376264 | tf_op jit(solution)/shard_map/ppermute | solution.py:16
  199.0 24.0 %collective-permute-start.19 = (bf16[128,4096]{1,0:T(8,128)(2,1)S(1)}, bf16[128,4096]{1,0:T(8,128)(2,1)S(1)}, u32[]{:S(2)}, u32[]{:S(2)}) collective-permute-start(bf16[128,4096]{1,0:T(8,128)(2,1)S(1)} %constant_dynamic-update-slice_fusion.2), channel_id=1, source_target_pairs={{0,2},{1,3},{2,0},{3,1},{4,6},{5,7},{6,4},{7,5},{8,10},{9,11},{10,... | collective-permute-start | bytes 3145736 | tf_op jit(solution)/shard_map/ppermute | solution.py:16
  216.9 7.3 %copy-start.17 = (f32[1,896]{1,0:T(1,128)S(1)}, f32[1,896]{1,0:T(1,128)}, u32[]{:S(2)}) copy-start(f32[1,896]{1,0:T(1,128)} %get-tuple-element.55) | copy-start | bytes 10756
  216.9 8.0 %copy-start.18 = (f32[1,896]{1,0:T(1,128)S(1)}, f32[1,896]{1,0:T(1,128)}, u32[]{:S(2)}) copy-start(f32[1,896]{1,0:T(1,128)} %get-tuple-element.64) | copy-start | bytes 10756
  217.0 13.2 %copy-start.24 = (bf16[256,896]{1,0:T(8,128)(2,1)}, bf16[256,896]{1,0:T(8,128)(2,1)S(1)}, u32[]{:S(2)}) copy-start(bf16[256,896]{1,0:T(8,128)(2,1)S(1)} %collective-permute-done.20.refs_8_.refs_12_) | copy-start | bytes 1376260
  218.9 11.4 %copy-start.25 = (bf16[256,896]{1,0:T(8,128)(2,1)}, bf16[256,896]{1,0:T(8,128)(2,1)S(1)}, u32[]{:S(2)}) copy-start(bf16[256,896]{1,0:T(8,128)(2,1)S(1)} %collective-permute-done.21.refs_9_.refs_13_) | copy-start | bytes 1376260
  223.0 7.2 %copy-start.5 = (bf16[256,4096]{1,0:T(8,128)(2,1)}, bf16[256,4096]{1,0:T(8,128)(2,1)S(1)}, u32[]{:S(2)}) copy-start(bf16[256,4096]{1,0:T(8,128)(2,1)S(1)} %constant_dynamic-update-slice_fusion.4.refs_0_) | copy-start | bytes 6291460
  223.0 36.1 %collective-permute-start.22 = (bf16[256,4096]{1,0:T(8,128)(2,1)S(1)}, bf16[256,4096]{1,0:T(8,128)(2,1)}, u32[]{:S(2)}, u32[]{:S(2)}) collective-permute-start(bf16[256,4096]{1,0:T(8,128)(2,1)S(1)} %constant_dynamic-update-slice_fusion.4.refs_0_), channel_id=1, source_target_pairs={{0,1},{1,0},{2,3},{3,2},{4,5},{5,4},{6,7},{7,6},{8,9},{9,8},{10,11... | collective-permute-start | bytes 6291464 | tf_op jit(solution)/shard_map/ppermute | solution.py:16
  277.3 13.7 %copy-start.13 = (f32[4,4096]{1,0:T(4,128)S(1)}, f32[4,4096]{1,0:T(4,128)}, u32[]{:S(2)}) copy-start(f32[4,4096]{1,0:T(4,128)} %get-tuple-element.82) | copy-start | bytes 196612
  277.3 14.9 %copy-start.14 = (f32[4,4096]{1,0:T(4,128)S(1)}, f32[4,4096]{1,0:T(4,128)}, u32[]{:S(2)}) copy-start(f32[4,4096]{1,0:T(4,128)} %get-tuple-element.75) | copy-start | bytes 196612
  277.3 14.9 %copy-start.15 = (f32[4,4096]{1,0:T(4,128)S(1)}, f32[4,4096]{1,0:T(4,128)}, u32[]{:S(2)}) copy-start(f32[4,4096]{1,0:T(4,128)} %get-tuple-element.76) | copy-start | bytes 196612
  277.3 14.9 %copy-start.16 = (f32[4,4096]{1,0:T(4,128)S(1)}, f32[4,4096]{1,0:T(4,128)}, u32[]{:S(2)}) copy-start(f32[4,4096]{1,0:T(4,128)} %get-tuple-element.77) | copy-start | bytes 196612
  277.3 15.3 %copy-start.10 = (f32[64,896]{1,0:T(8,128)S(1)}, f32[64,896]{1,0:T(8,128)}, u32[]{:S(2)}) copy-start(f32[64,896]{1,0:T(8,128)} %get-tuple-element.78) | copy-start | bytes 688132
  277.3 16.7 %copy-start.7 = (f32[64,896]{1,0:T(8,128)S(1)}, f32[64,896]{1,0:T(8,128)}, u32[]{:S(2)}) copy-start(f32[64,896]{1,0:T(8,128)} %get-tuple-element.53) | copy-start | bytes 688132
  277.3 16.7 %copy-start.8 = (f32[64,896]{1,0:T(8,128)S(1)}, f32[64,896]{1,0:T(8,128)}, u32[]{:S(2)}) copy-start(f32[64,896]{1,0:T(8,128)} %get-tuple-element.61) | copy-start | bytes 688132
  277.3 16.7 %copy-start.9 = (f32[64,896]{1,0:T(8,128)S(1)}, f32[64,896]{1,0:T(8,128)}, u32[]{:S(2)}) copy-start(f32[64,896]{1,0:T(8,128)} %get-tuple-element.74) | copy-start | bytes 688132
  293.6 6.7 %collective-permute-start.25 = (f32[2,2,8,1152]{3,2,1,0:T(8,128)S(1)}, f32[2,2,8,1152]{3,2,1,0:T(8,128)S(1)}, u32[]{:S(2)}, u32[]{:S(2)}) collective-permute-start(f32[2,2,8,1152]{3,2,1,0:T(8,128)S(1)} %fusion.3), channel_id=1, source_target_pairs={{0,4},{4,0},{8,12},{12,8},{16,20},{20,16},{24,28},{28,24},{1,5},{5... | collective-permute-start | bytes 442376 | tf_op jit(solution)/shard_map/ppermute | solution.py:16
  294.1 8.7 %collective-permute-start.23 = (f32[2,2,8,1152]{3,2,1,0:T(8,128)S(1)}, f32[2,2,8,1152]{3,2,1,0:T(8,128)S(1)}, u32[]{:S(2)}, u32[]{:S(2)}) collective-permute-start(f32[2,2,8,1152]{3,2,1,0:T(8,128)S(1)} %fusion.11), channel_id=1, source_target_pairs={{0,4},{4,0},{8,12},{12,8},{16,20},{20,16},{24,28},{28,24},{1,5},{5... | collective-permute-start | bytes 442376 | tf_op jit(solution)/shard_map/ppermute | solution.py:16
  300.4 8.3 %collective-permute-start.26 = (f32[2,8,1152]{2,1,0:T(8,128)S(1)}, f32[2,8,1152]{2,1,0:T(8,128)S(1)}, u32[]{:S(2)}, u32[]{:S(2)}) collective-permute-start(f32[2,8,1152]{2,1,0:T(8,128)S(1)} %dynamic-slice_bitcast_fusion.1), channel_id=1, source_target_pairs={{0,16},{4,20},{8,24},{12,28},{16,0},{20,4},{24,8},{28,12},{1,17},{... | collective-permute-start | bytes 221192 | tf_op jit(solution)/shard_map/ppermute | solution.py:16
  302.9 7.1 %collective-permute-start.24 = (f32[2,8,1152]{2,1,0:T(8,128)S(1)}, f32[2,8,1152]{2,1,0:T(8,128)S(1)}, u32[]{:S(2)}, u32[]{:S(2)}) collective-permute-start(f32[2,8,1152]{2,1,0:T(8,128)S(1)} %dynamic-slice_bitcast_fusion.2), channel_id=1, source_target_pairs={{0,16},{4,20},{8,24},{12,28},{16,0},{20,4},{24,8},{28,12},{1,17},{... | collective-permute-start | bytes 221192 | tf_op jit(solution)/shard_map/ppermute | solution.py:16
  311.2 7.4 %collective-permute-start.27 = (f32[8,1792]{1,0:T(8,128)S(1)}, f32[8,1792]{1,0:T(8,128)S(1)}, u32[]{:S(2)}, u32[]{:S(2)}) collective-permute-start(f32[8,1792]{1,0:T(8,128)S(1)} %fusion.13), channel_id=1, source_target_pairs={{0,8},{4,12},{8,0},{12,4},{16,24},{20,28},{24,16},{28,20},{1,9},{5... | collective-permute-start | bytes 172040 | tf_op jit(solution)/shard_map/ppermute | solution.py:16
  315.8 11.3 %all-to-all-start.1 = ((f32[32,1,1152]{2,1,0:T(1,128)}), f32[32,1,1152]{2,1,0:T(1,128)S(1)}, u32[]{:S(2)}, u32[]{:S(2)}) async-start(f32[32,1,1152]{2,1,0:T(1,128)} %all_to_all.25), calls=%async_computation.1 | async-start | bytes 294912 | tf_op jit(solution)/shard_map/all_to_all | solution.py:428
